TPU v7x, 128 devices: a whole 4x4x4 slice. The times are simulated.
128 devices in a mesh: clique: 32 (over y, z, core), subtree: 4 (over x).
Axes of the slice: x: 4, y: 4, z: 4, core: 2. Of those that a mesh axis runs over, the one named last changes fastest.
Arguments:
- potentials: float32 [4, 32, 1024, 1024], P('subtree', 'clique'), may hold values from -125 to 125
- parent: int32 [4, 32], P('subtree'), may hold values from 0 to 31, as said below
- child_drop: int32 [4, 32], replicated, may hold values from 0 to 3
- parent_drop: int32 [4, 32], replicated, may hold values from 0 to 3
Outputs:
- log_marginals: float32 [4, 32, 1024, 1024], P('subtree', 'clique')
Inputs may be any that keep to these rules, and one draw needn't show every extreme that they name: parent[s, 0] = 0 marks the root of subtree s; every other clique's parent is a clique of the same subtree, and following parents from any clique reaches clique 0 in at most 2 steps.
All inputs are finite; a program needn't handle non-finite values.
Results may differ from a plain program's by a relative error of at most 0.0003.
Values sent between devices are 32-bit elements; how exact they have to be, the bound alone decides.
A program may use at most 192 MiB of HBM per device.

v0:
```python
import jax
import jax.numpy as jnp
from jax import lax
from jax.sharding import PartitionSpec as P

LEVELS = 32
DEPTH = 2


def shifted(value, axis, steps):
    count = lax.axis_size(axis)
    initial, last = (max(0, -steps), min(count, count - steps))
    return lax.ppermute(value, axis, [(source, source + steps) for source in range(initial, last)])


def spread_slots(slot_tables, levels):
    number = slot_tables.shape[0]
    squared = levels * levels
    over_first = slot_tables[:, 0].reshape(number, 1, levels, squared)
    over_second = slot_tables[:, 1].reshape(number, levels, 1, squared)
    front = (over_first + over_second).reshape(number, squared, squared)
    columns = lax.broadcasted_iota(jnp.int32, (2 * levels, squared), 1)
    picks = lax.broadcasted_iota(jnp.int32, (2 * levels, squared), 0)
    spread_table = jnp.where(
        picks < levels, columns % levels == picks, columns // levels == picks - levels
    ).astype(jnp.float32)
    back_slots = jnp.concatenate(
        [
            slot_tables[:, 2].reshape(number, squared, levels),
            slot_tables[:, 3].reshape(number, squared, levels),
        ],
        axis=2,
    )
    back = jnp.einsum(
        "nab,bc->nac",
        back_slots,
        spread_table,
        precision=lax.Precision.HIGHEST,
        preferred_element_type=jnp.float32,
    )
    return front + back


def one_hot_four(dropped):
    return (dropped[:, None] == jnp.arange(4)[None, :]).astype(jnp.float32)


def slotted(message, dropped):
    return one_hot_four(dropped)[:, :, None] * message[:, None, :]


def log_sum(stacked, axis):
    top = jnp.max(stacked, axis=axis, keepdims=True)
    return jnp.squeeze(top, axis) + jnp.log(jnp.sum(jnp.exp(stacked - top), axis=axis))


def margin_first(table):
    levels = LEVELS
    return log_sum(table.reshape(levels, levels, levels * levels), 0).reshape(levels**3)


def margin_second(table):
    levels = LEVELS
    return log_sum(table.reshape(levels, levels, levels * levels), 1).reshape(levels**3)


def margin_third(table):
    levels = LEVELS
    return log_sum(table.T.reshape(levels, levels, levels * levels), 0).T.reshape(levels**3)


def margin_fourth(table):
    levels = LEVELS
    return log_sum(table.T.reshape(levels, levels, levels * levels), 1).T.reshape(levels**3)


def all_margins(table):
    levels = LEVELS
    squared = levels * levels
    by_rows = table.reshape(levels, levels, squared)
    by_cols = table.T.reshape(levels, levels, squared)
    parts = [
        log_sum(by_rows, 0).reshape(levels**3),
        log_sum(by_rows, 1).reshape(levels**3),
        log_sum(by_cols, 0).T.reshape(levels**3),
        log_sum(by_cols, 1).T.reshape(levels**3),
    ]
    return jnp.stack(parts)


def margins(tables):
    return lax.map(all_margins, tables)


def picked_margins(tables, dropped):

    def one_clique(pair):
        return lax.switch(
            pair[1], [margin_first, margin_second, margin_third, margin_fourth], pair[0]
        )

    return lax.map(one_clique, (tables, dropped))


def per_device(potentials, parent, child_drop, parent_drop):
    local_count = potentials.shape[1]
    squared = potentials.shape[2]
    levels = LEVELS
    cubed = levels**3
    total_cliques = local_count * lax.axis_size("clique")
    subtree_count = lax.axis_size("subtree")
    first_clique = lax.axis_index("clique") * local_count
    subtree_here = lax.axis_index("subtree")
    subtree_next = jnp.minimum(subtree_here + 1, subtree_count - 1)
    tables = potentials.reshape(local_count, squared, squared)
    parents_all = parent[0]
    child_row = lax.dynamic_slice_in_dim(child_drop, subtree_here, 1, 0)[0]
    parent_row = lax.dynamic_slice_in_dim(parent_drop, subtree_here, 1, 0)[0]
    next_pdrop = lax.dynamic_slice_in_dim(parent_drop, subtree_next, 1, 0)[0][:1]
    targets = parents_all * 4 + parent_row
    positions = jnp.arange(total_cliques, dtype=jnp.int32)
    own_positions = first_clique + jnp.arange(local_count, dtype=jnp.int32)
    own_parent = lax.dynamic_slice_in_dim(parents_all, first_clique, local_count)
    own_cdrop = lax.dynamic_slice_in_dim(child_row, first_clique, local_count)
    own_pdrop = lax.dynamic_slice_in_dim(parent_row, first_clique, local_count)
    own_targets = own_parent * 4 + own_pdrop
    slot_rows = first_clique * 4 + jnp.arange(4 * local_count, dtype=jnp.int32)
    incidence = ((targets[None, :] == slot_rows[:, None]) & (positions[None, :] != 0)).astype(
        jnp.float32
    )
    incoming = jnp.zeros((local_count, 4, cubed), jnp.float32)
    for iteration in range(DEPTH):
        upward = tables + spread_slots(incoming, levels)
        message = picked_margins(upward, own_cdrop)
        add_arrived = jax.tree.map(
            lambda a: lax.all_gather(a, "clique", axis=0, tiled=True), message
        )
        add_columns = lax.slice_in_dim(incidence, 0, add_arrived.shape[0], axis=1)
        summed = jnp.zeros((4 * local_count, cubed), jnp.float32) + jnp.dot(
            add_columns,
            add_arrived,
            precision=lax.Precision.HIGHEST,
            preferred_element_type=jnp.float32,
        )
        incoming = summed.reshape(local_count, 4, cubed)
    upward = tables + spread_slots(incoming, levels)
    message = picked_margins(upward, own_cdrop)
    holds_root = (lax.axis_index("clique") == 0).astype(jnp.float32)
    below_top = (subtree_here > 0).astype(jnp.float32)
    root_in = jnp.zeros((1, 4, cubed), jnp.float32)
    for iteration in range(subtree_count):
        root_up = upward + spread_slots(root_in, levels)
        root_message = picked_margins(root_up, own_cdrop)
        if iteration + 1 < subtree_count:
            arrived = shifted(root_message, "subtree", -1)
            root_in = holds_root * slotted(arrived, next_pdrop)
    root_belief = root_up
    for iteration in range(subtree_count - 1):
        outgoing = picked_margins(root_belief, next_pdrop)
        received = shifted(outgoing, "subtree", 1)
        correction = received - root_message
        root_belief = root_up + below_top * spread_slots(slotted(correction, own_cdrop), levels)
    is_root = own_positions == 0
    belief = jnp.where(is_root[:, None, None], root_belief, upward)
    for iteration in range(DEPTH):
        chooser = (
            jnp.arange(4 * total_cliques, dtype=jnp.int32)[None, :] == own_targets[:, None]
        ).astype(jnp.float32)

        def add_parents(arrived, offset):
            rows_count = arrived.shape[0]
            columns = lax.dynamic_slice_in_dim(chooser, offset * 4, rows_count * 4, 1)
            return jnp.dot(
                columns,
                arrived.reshape(rows_count * 4, cubed),
                precision=lax.Precision.HIGHEST,
                preferred_element_type=jnp.float32,
            )

        received = add_parents(
            lax.all_gather(margins(belief), "clique", axis=0, tiled=True), jnp.int32(0)
        )
        updated = upward + spread_slots(slotted(received - message, own_cdrop), levels)
        belief = jnp.where(is_root[:, None, None], belief, updated)
    belief_top = jnp.max(belief, axis=(1, 2), keepdims=True)
    log_total = belief_top + jnp.log(
        jnp.sum(jnp.exp(belief - belief_top), axis=(1, 2), keepdims=True)
    )
    return (belief - log_total).reshape(1, local_count, squared, squared)


def solution(mesh):
    placed = (P("subtree", "clique", None, None), P("subtree", None), P(), P())
    return jax.shard_map(
        per_device,
        mesh=mesh,
        in_specs=placed,
        out_specs=P("subtree", "clique", None, None),
        check_vma=False,
    )
```

profile of v0, /device:TPU:1, one launch (start us, length us, event | category | flops | bytes accessed | tf_op | source)
XLA Modules:
  0.0 636.4 jit_solution(6805025038921047938)
XLA Ops:
  8.4 7.4 %bitcast_add_fusion.13 = (f32[1024,1024]{1,0:T(8,128)}, f32[1024,1024]{1,0:T(8,128)}) fusion(f32[1,1,1024,1024]{3,2,1,0:T(8,128)} %param.44, s32[64]{0:T(128)S(1)} %iota_add_fusion, s32[1024]{0:T(1024)S(1)} %get-tuple-element.380, s32[1024]{0:T(1024)S(1)} %get-tuple-element.383, s32[1024]{0:T(1024)S(1)} %get-tuple-element.381, ...), kind=kOutput, calls=%fused_computation.189 | convolution fusion | flops 806682624 | bytes 12601664 | tf_op jit(solution)/shard_map/nab,bc->nac/dot_general | solution.py:34
  15.8 11.0 %conditional.10 = (f32[32768]{0:T(1024)S(1)}) conditional(s32[]{:T(128)} %clamp.32, f32[1024,1024]{1,0:T(8,128)} %get-tuple-element.370, f32[1024,1024]{1,0:T(8,128)} %get-tuple-element.370, f32[1024,1024]{1,0:T(8,128)} %get-tuple-element.370, f32[1024,1024]{1,0:T(8,128)} %get-tuple-element.370), branch_computations={%region_0.3_spmd, %region_3.6_spmd, %region_6.9_spmd, %region_9.12... | conditional | flops 3112960 | bytes 34865188 | solution.py:98
  15.8 5.4 copy.125
  27.8 49.3 %all-gather.11.cloned.1.call-done = f32[1048576]{0:T(1024)} async-done(((f32[32768]{0:T(1024)}), f32[1048576]{0:T(1024)}) %all-gather.11.cloned.1.call-update) | async-done | bytes 4194320 | tf_op jit(solution)/shard_map/all_gather | solution.py:136
  94.2 11.2 %conditional.11 = (f32[32768]{0:T(1024)S(1)}) conditional(s32[]{:T(128)} %clamp.32, f32[1024,1024]{1,0:T(8,128)} %fusion.61, f32[1024,1024]{1,0:T(8,128)} %fusion.61, f32[1024,1024]{1,0:T(8,128)} %fusion.61, f32[1024,1024]{1,0:T(8,128)} %fusion.61), branch_computations={%region_12.15_spmd, %region_15.18_spmd, %region_18.21_spmd, %regio... | conditional | flops 3112960 | bytes 34865188 | solution.py:98
  106.1 45.7 %all-gather.13.cloned.1.call-done = f32[1048576]{0:T(1024)} async-done(((f32[32768]{0:T(1024)}), f32[1048576]{0:T(1024)}) %all-gather.13.cloned.1.call-update) | async-done | bytes 4194320 | tf_op jit(solution)/shard_map/all_gather | solution.py:136
  164.5 8.1 %fusion.133 = (f32[1024,1024]{1,0:T(8,128)}, f32[1024,1024]{1,0:T(8,128)}) fusion(f32[1024,1024]{1,0:T(8,128)} %get-tuple-element.371, s32[64]{0:T(128)S(1)} %iota_add_fusion, s32[1024]{0:T(1024)S(1)} %get-tuple-element.380, s32[1024]{0:T(1024)S(1)} %get-tuple-element.383, s32[1024]{0:T(1024)S(1)} %get-tuple-element.381, s32[1024]{0:T(1024)S(1)} %get-tuple-element.382, ...), kind=kOutput, calls=%fused_computation.354 | convolution fusion | flops 808845312 | bytes 21252416 | tf_op jit(solution)/shard_map/nab,bc->nac/dot_general | solution.py:34
  172.6 19.5 %conditional.12 = (f32[32768]{0:T(1024)S(1)}) conditional(s32[]{:T(128)} %clamp.32, f32[1024,1024]{1,0:T(8,128)} %get-tuple-element.372, f32[1024,1024]{1,0:T(8,128)} %get-tuple-element.372, f32[1024,1024]{1,0:T(8,128)} %get-tuple-element.372, f32[1024,1024]{1,0:T(8,128)} %get-tuple-element.372), branch_computations={%region_24.27_spmd, %region_27.30_spmd, %region_30.33_spmd, %regio... | conditional | flops 3112960 | bytes 34865188 | solution.py:98
  206.4 11.0 %conditional.13 = (f32[32768]{0:T(1024)S(1)}) conditional(s32[]{:T(128)} %clamp.32, f32[1024,1024]{1,0:T(8,128)} %fusion.59, f32[1024,1024]{1,0:T(8,128)} %fusion.59, f32[1024,1024]{1,0:T(8,128)} %fusion.59, f32[1024,1024]{1,0:T(8,128)} %fusion.59), branch_computations={%region_36.39_spmd, %region_39.42_spmd, %region_42.45_spmd, %regio... | conditional | flops 3112960 | bytes 34865188 | solution.py:98
  231.7 11.0 %conditional.14 = (f32[32768]{0:T(1024)S(1)}) conditional(s32[]{:T(128)} %clamp.32, f32[1024,1024]{1,0:T(8,128)} %fusion.58, f32[1024,1024]{1,0:T(8,128)} %fusion.58, f32[1024,1024]{1,0:T(8,128)} %fusion.58, f32[1024,1024]{1,0:T(8,128)} %fusion.58), branch_computations={%region_48.51_spmd, %region_51.54_spmd, %region_54.57_spmd, %regio... | conditional | flops 3112960 | bytes 34865188 | solution.py:98
  244.2 5.6 collective-permute-done.2
  273.3 5.9 conditional.16
  287.9 13.5 %conditional.17 = (f32[32768]{0:T(1024)S(1)}) conditional(s32[]{:T(128)} %clamp.33, f32[1024,1024]{1,0:T(8,128)} %fusion.56, f32[1024,1024]{1,0:T(8,128)} %fusion.56, f32[1024,1024]{1,0:T(8,128)} %fusion.56, f32[1024,1024]{1,0:T(8,128)} %fusion.56), branch_computations={%region_84.87_spmd, %region_87.90_spmd, %region_90.93_spmd, %regio... | conditional | flops 3112960 | bytes 34865188 | solution.py:98
  311.5 22.6 %conditional.18 = (f32[32768]{0:T(1024)S(1)}) conditional(s32[]{:T(128)} %clamp.33, (f32[1024,1024]{1,0:T(8,128)}, f32[]{:T(128)}, f32[1,4,32768]{2,1,0:T(4,128)S(1)}, f32[1024,1024]{1,0:T(8,128)}, f32[1,4,32768]{2,1,0:T(4,128)S(1)}) %tuple.163, (f32[1024,1024]{1,0:T(8,128)}, f32[]{:T(128)}, ...), branch_computations={%region_96.99_spmd, %region_99.102_spmd, %region_102.105_spmd, %re... | conditional | flops 7307264 | bytes 73924680 | solution.py:98
  314.5 5.5 fusion.37
  344.8 7.0 %bitcast_reduce_fusion.23 = (f32[32,1024]{1,0:T(8,128)S(1)}, f32[1024,1024]{1,0:T(8,128)}) fusion(f32[1024,1024]{1,0:T(8,128)} %get-tuple-element.373, f32[1024,1024]{1,0:T(8,128)S(1)} %copy-done.1, s32[64]{0:T(128)S(1)} %iota_add_fusion, s32[1024]{0:T(1024)S(1)} %get-tuple-element.380, s32[1024]{0:T(1024)S(1)} %get-tuple-element.383, ...), kind=kOutput, calls=%fused_computation.342 | convolution fusion | flops 810909696 | bytes 17189188 | tf_op jit(solution)/shard_map/nab,bc->nac/dot_general | solution.py:34
  379.3 11.5 %conditional.19 = (f32[32768]{0:T(1024)S(1)}) conditional(s32[]{:T(128)} %clamp.32, f32[1024,1024]{1,0:T(8,128)} %get-tuple-element.373, f32[1024,1024]{1,0:T(8,128)} %get-tuple-element.373, (f32[1024,1024]{1,0:T(8,128)}) %tuple.166, (f32[1024,1024]{1,0:T(8,128)}) %tuple.166), branch_computations={%region_116.119_spmd, %region_119.122_spmd, %region_122.125_spmd, ... | conditional | flops 3112960 | bytes 34865188 | solution.py:98
  390.8 57.0 %all-gather.15.cloned.1.call-done = f32[32,4,32768]{2,1,0:T(4,128)} async-done(((f32[1,4,32768]{2,1,0:T(4,128)}), f32[32,4,32768]{2,1,0:T(4,128)}) %all-gather.15.cloned.1.call-update) | async-done | bytes 16777232 | tf_op jit(solution)/shard_map/all_gather | solution.py:181
  447.8 19.4 %reshape.1248 = f32[128,32768]{1,0:T(8,128)} reshape(f32[32,4,32768]{2,1,0:T(4,128)} %all-gather.15.cloned.1.call-done) | data formatting | bytes 33554432
  467.2 9.0 %fusion.94 = f32[1,32768]{1,0:T(1,128)S(1)} fusion(f32[128,32768]{1,0:T(8,128)} %reshape.1248, s32[]{:T(128)} %bitcast.135), kind=kOutput, calls=%fused_computation.313 | convolution fusion | flops 50331776 | bytes 16908292 | tf_op jit(solution)/shard_map/dot_general | solution.py:173
  492.7 5.6 copy.146
  510.0 72.2 %all-gather.17.cloned.1.call-done = f32[32,4,32768]{2,1,0:T(4,128)} async-done(((f32[1,4,32768]{2,1,0:T(4,128)}), f32[32,4,32768]{2,1,0:T(4,128)}) %all-gather.17.cloned.1.call-update) | async-done | bytes 16777232 | tf_op jit(solution)/shard_map/all_gather | solution.py:181
  582.2 19.4 %reshape.1250 = f32[128,32768]{1,0:T(8,128)} reshape(f32[32,4,32768]{2,1,0:T(4,128)} %all-gather.17.cloned.1.call-done) | data formatting | bytes 33554432
  601.6 9.3 %fusion.92 = f32[1,32768]{1,0:T(1,128)S(1)} fusion(f32[128,32768]{1,0:T(8,128)} %reshape.1250, s32[]{:T(128)} %bitcast.135), kind=kOutput, calls=%fused_computation.311 | convolution fusion | flops 50331776 | bytes 16908292 | tf_op jit(solution)/shard_map/dot_general | solution.py:173
  (251 shorter events, 271.4 us)
Async XLA Ops:
  6.5 70.6 %all-gather.11.cloned.1.call-start = ((), (), s32[]{:S(2)}) async-start(), calls=%async_computation | async-start | bytes 4325376 | tf_op jit(solution)/shard_map/all_gather | solution.py:136
  15.8 12.0 %copy-start.33 = (s32[4,32]{1,0:T(4,128)S(1)}, s32[4,32]{1,0:T(4,128)}, u32[]{:S(2)}) copy-start(s32[4,32]{1,0:T(4,128)} %param.47) | copy-start | bytes 1540
  15.8 12.0 %copy-start.34 = (s32[1,32]{1,0:T(1,128)S(1)}, s32[1,32]{1,0:T(1,128)}, u32[]{:S(2)}) copy-start(s32[1,32]{1,0:T(1,128)} %param.45) | copy-start | bytes 388
  27.5 124.3 %all-gather.13.cloned.1.call-start = ((), (), s32[]{:S(2)}) async-start(), calls=%async_computation.1 | async-start | bytes 4325376 | tf_op jit(solution)/shard_map/all_gather | solution.py:136
  87.6 2.2 copy-start.20
  106.1 341.7 %all-gather.15.cloned.1.call-start = ((), (), s32[]{:S(2)}) async-start(), calls=%async_computation.2 | async-start | bytes 17301504 | tf_op jit(solution)/shard_map/all_gather | solution.py:181
  162.3 2.2 copy-start.21
  192.0 5.7 collective-permute-start
  199.8 2.2 copy-start.8
  217.3 5.7 collective-permute-start.1
  225.1 2.2 copy-start.9
  242.6 7.1 %collective-permute-start.2 = (f32[1,32768]{1,0:T(1,128)S(1)}, f32[1,32768]{1,0:T(1,128)S(1)}, u32[]{:S(2)}, u32[]{:S(2)}) collective-permute-start(f32[1,32768]{1,0:T(1,128)S(1)} %bitcast.560), channel_id=1, source_target_pairs={{1,0},{2,1},{3,2},{5,4},{6,5},{7,6},{9,8},{10,9},{11,10},{13,12},{... | collective-permute-start | bytes 393224 | tf_op jit(solution)/shard_map/ppermute | solution.py:13
  269.0 10.3 %collective-permute-start.3 = (f32[1,32768]{1,0:T(1,128)S(1)}, f32[1,32768]{1,0:T(1,128)S(1)}, u32[]{:S(2)}, u32[]{:S(2)}) collective-permute-start(f32[1,32768]{1,0:T(1,128)S(1)} %bitcast.563), channel_id=1, source_target_pairs={{0,1},{1,2},{2,3},{4,5},{5,6},{6,7},{8,9},{9,10},{10,11},{12,13},{... | collective-permute-start | bytes 393224 | tf_op jit(solution)/shard_map/ppermute | solution.py:13
  281.4 2.2 copy-start
  301.4 5.0 collective-permute-start.4
  312.3 2.2 copy-start.4
  334.1 6.3 collective-permute-start.5
  342.6 2.2 copy-start.1
  354.3 3.5 copy-start.16
  369.7 3.5 copy-start.19
  373.2 4.4 copy-start.35
  376.1 206.1 %all-gather.17.cloned.1.call-start = ((), (), s32[]{:S(2)}) async-start(), calls=%async_computation.3 | async-start | bytes 17301504 | tf_op jit(solution)/shard_map/all_gather | solution.py:181
  488.0 3.5 copy-start.17
  503.7 3.5 copy-start.18
  (6 other events, 9.9 us)
Sparse Core Ops, SparseCore 0:
  27.6 49.4 all-gather.10
  106.2 45.5 all-gather.12
  376.2 71.6 all-gather.14
  510.1 71.9 all-gather.16
where the time goes:
time: 647 us; the launch traced here: 636 us
  waiting for transfers between devices  243 us (38%)
  local copies, waits for them, and re-layouts  143 us (22%)
  other arithmetic  108 us (17%)
  matrix products  82.6 us (13%)
  loops' own time  26.5 us (4%)
  between operations  17.8 us (3%)
  starting transfers between devices  14.8 us (2%)
    all_gather x2, waiting for transfers between devices, per_device(): lax.all_gather(margins(belief), 'clique', axis=0, tiled=True)  129 us
    all_gather x2, waiting for transfers between devices, per_device(): lax.all_gather(a, 'clique', axis=0, tiled=True)  95 us
    unnamed x44, local copies, waits for them, and re-layouts  58.3 us
    dot_general x11, matrix products, spread_slots(): jnp.einsum('nab,bc->nac', back_slots, spread_table, precision=lax.Precisi...  57 us
    reduce_sum x18, other arithmetic, log_sum(): jnp.sum(jnp.exp(stacked - top), axis=axis)  43.7 us
    reduce_max x16, other arithmetic, log_sum(): top = jnp.max(stacked, axis=axis, keepdims=True)  40.1 us
    add x5, local copies, waits for them, and re-layouts  26.8 us
    another operation x10, loops' own time, one_clique(): lax.switch(pair[1], [margin_first, margin_second, margin_third, margin_fo...  26.5 us
  transfers between devices with their start and end apart: 10, of which 9 were waited for; matrix products, arithmetic and copies ran while one was open for 3% of the time, Pallas kernels for 0%

commit v1 on v0

v1 whole, which is shorter than its diff:
```python
import functools

import jax
import jax.numpy as jnp
from jax import lax
from jax.experimental import pallas as pl
from jax.experimental.pallas import tpu as pltpu
from jax.sharding import PartitionSpec as P

PIECES = 32
CHUNKS = 8
MESH = pl.DeviceIdType.MESH
F32 = jnp.float32
VMEM = pltpu.VMEM
SMEM = pltpu.SMEM


def lanes():
    return lax.broadcasted_iota(jnp.int32, (8, 128), 1)


def rows():
    return lax.broadcasted_iota(jnp.int32, (8, 128), 0)


def take(vec, index):
    return jnp.take_along_axis(vec, index, axis=1, mode="promise_in_bounds")


def tree(parts, op):
    parts = list(parts)
    while len(parts) > 1:
        parts = [op(*parts[n : n + 2]) if n + 1 < len(parts) else parts[n] for n in range(0, len(parts), 2)]
    return parts[0]


def tile(table, a0, i, t):
    return table[pl.ds(pl.multiple_of(a0 * 32 + 8 * i, 8), 8), 128 * t : 128 * (t + 1)]


def placed(slots, a0, base=None):
    lane, row = lanes(), rows()
    a0_tile, a0_row = a0 // 8, a0 % 8

    def slot_row(k, j):
        return slots[a0_tile * 8 + j, k, pl.ds(a0_row, 1), :]

    second = [slot_row(1, t) for t in range(8)]
    out = []
    for i in range(4):
        both = [jnp.where(row < 4, slot_row(k, 2 * i), slot_row(k, 2 * i + 1)) for k in (2, 3)]
        third = take(both[0], (row % 4) * 32 + lane % 32)
        out.append(
            [
                (slots[i * 8 + t, 0] + second[t])
                + (third + take(both[1], (row % 4) * 32 + lane // 32 + 4 * t))
                for t in range(8)
            ]
        )
    return out


def margin_0(table, store):
    def body(i, carry):
        for t in range(8):
            parts = [tile(table, a0, i, t) for a0 in range(32)]
            top = tree(parts, jnp.maximum)
            total = tree([jnp.exp(part - top) for part in parts], jnp.add)
            store(i * 8 + t, None, top + jnp.log(total))
        return carry

    lax.fori_loop(0, 4, body, 0)


def margin_1(table, store):
    def over_rows(vec, op):
        for shift in (4, 2, 1):
            vec = op(vec, pltpu.roll(vec, shift, 0))
        return vec

    def body(a0, carry):
        for t in range(8):
            parts = [tile(table, a0, i, t) for i in range(4)]
            top = over_rows(tree(parts, jnp.maximum), jnp.maximum)
            total = over_rows(tree([jnp.exp(part - top) for part in parts], jnp.add), jnp.add)
            store((a0 // 8) * 8 + t, a0 % 8, (top + jnp.log(total))[0:1])
        return carry

    lax.fori_loop(0, 32, body, 0)


def store_packed(result, a0, i, store):
    packed = jnp.where(lanes() // 32 == rows() % 4, result, 0.0)
    packed = packed + pltpu.roll(packed, 1, 0)
    packed = packed + pltpu.roll(packed, 2, 0)
    store((a0 // 8) * 8 + 2 * i, a0 % 8, packed[3:4])
    store((a0 // 8) * 8 + 2 * i + 1, a0 % 8, packed[7:8])


def margin_2(table, store):
    def over_groups(vec, op):
        for shift in (64, 32):
            vec = op(vec, pltpu.roll(vec, shift, 1))
        return vec

    def body(a0, carry):
        for i in range(4):
            parts = [tile(table, a0, i, t) for t in range(8)]
            top = over_groups(tree(parts, jnp.maximum), jnp.maximum)
            total = over_groups(tree([jnp.exp(part - top) for part in parts], jnp.add), jnp.add)
            store_packed(top + jnp.log(total), a0, i, store)
        return carry

    lax.fori_loop(0, 32, body, 0)


def margin_3(table, store):
    lane = lanes()

    def over_lanes(parts, op):
        parts = list(parts)
        for shift in (16, 8, 4):
            upper = (lane & shift) != 0
            half = len(parts) // 2
            parts = [
                op(
                    jnp.where(upper, high, low),
                    take(jnp.where(upper, low, high), lane ^ shift),
                )
                for low, high in zip(parts[:half], parts[half:])
            ]
        vec = parts[0]
        for shift in (2, 1):
            vec = op(vec, take(vec, lane ^ shift))
        return vec

    def body(a0, carry):
        for i in range(4):
            parts = [tile(table, a0, i, t) for t in range(8)]
            top = over_lanes(parts, jnp.maximum)
            total = over_lanes(
                [jnp.exp(part - take(top, (lane // 32) * 32 + 4 * t)) for t, part in enumerate(parts)],
                jnp.add,
            )
            level = lane % 32
            result = take(top + jnp.log(total), (level % 4) * 32 + (level // 4) * 4)
            store_packed(result, a0, i, store)
        return carry

    lax.fori_loop(0, 32, body, 0)


MARGINS = (margin_0, margin_1, margin_2, margin_3)


def message_store(message):
    def store(piece, row, value):
        if row is None:
            message[piece] = value
        else:
            message[piece, pl.ds(row, 1), :] = value

    return store


def slot_store(slots, k):
    def store(piece, row, value):
        if row is None:
            slots[piece, k] = value
        else:
            slots[piece, k, pl.ds(row, 1), :] = value

    return store


def chosen_margin(table, axis, message):
    for k in range(4):

        @pl.when(axis == k)
        def _(k=k):
            MARGINS[k](table, message_store(message))


def chunk_copy(source, table, sems, chunk):
    size = 1024 // CHUNKS
    part = pl.ds(pl.multiple_of(chunk * size, size), size)
    return pltpu.make_async_copy(source.at[part], table.at[part], sems.at[chunk])


def load(potentials, table, sems):
    for chunk in range(CHUNKS):
        chunk_copy(potentials, table, sems, chunk).start()


def wait_load(potentials, table, sems):
    for chunk in range(CHUNKS):
        chunk_copy(potentials, table, sems, chunk).wait()


def place_all(potentials, table, sems, slots, after=None):
    per_chunk = 32 // CHUNKS

    def chunk_body(chunk, carry):
        chunk_copy(potentials, table, sems, chunk).wait()

        def body(n, inner):
            a0 = chunk * per_chunk + n
            add = placed(slots, a0)
            for i in range(4):
                for t in range(8):
                    where = pl.ds(pl.multiple_of(a0 * 32 + 8 * i, 8), 8)
                    table[where, 128 * t : 128 * (t + 1)] = tile(table, a0, i, t) + add[i][t]
            return inner

        lax.fori_loop(0, per_chunk, body, 0)
        if after is not None:
            after(chunk)
        return carry

    lax.fori_loop(0, CHUNKS, chunk_body, 0)


def add_slot(slots, k, message, minus=None, shift=None):
    def body(piece, carry):
        value = message[piece]
        if minus is not None:
            value = value - minus[piece]
        if shift is not None:
            value = value - shift
        slots[piece, k] = slots[piece, k] + value
        return carry

    lax.fori_loop(0, PIECES, body, 0)


def copy_slots(source, target):
    def body(piece, carry):
        for k in range(4):
            target[piece, k] = source[piece, k]
        return carry

    lax.fori_loop(0, PIECES, body, 0)


def first_kernel(parent, child_drop, parent_drop, potentials, message, previous, last, table, sems):
    me, tree_here = lax.axis_index("clique"), lax.axis_index("subtree")
    load(potentials, table, sems)

    def clear(n, carry):
        last[n] = PIECES
        return carry

    lax.fori_loop(0, 128, clear, 0)
    previous[0] = PIECES

    def link(c, carry):
        target = parent[0, c] * 4 + parent_drop[tree_here, c]
        previous[c] = last[target]
        last[target] = c
        return carry

    lax.fori_loop(1, PIECES, link, 0)
    wait_load(potentials, table, sems)
    chosen_margin(table, child_drop[tree_here, me], message)


def up_kernel(child_drop, potentials, slots, message, table, sems):
    me, tree_here = lax.axis_index("clique"), lax.axis_index("subtree")
    load(potentials, table, sems)
    place_all(potentials, table, sems, slots)
    chosen_margin(table, child_drop[tree_here, me], message)


def chain_slot(step, s, child_drop, parent_drop):
    from_next = parent_drop[jnp.minimum(s + 1, 3), 0]
    from_previous = child_drop[s, 0]
    if step == 1:
        return jnp.where(s == 2, from_next, from_previous)
    if step == 2:
        return jnp.where(s == 1, from_next, from_previous)
    return jnp.where(s == 0, from_next, from_previous)


def chain_kernel(step, *refs):
    child_drop, parent_drop, potentials, slots = refs[:4]
    message, table, held, sems = refs[-4:]
    s = lax.axis_index("subtree")
    load(potentials, table, sems)
    to_next = parent_drop[jnp.minimum(s + 1, 3), 0]
    to_previous = child_drop[s, 0]
    axis = jnp.where(s == {1: 0, 2: 1, 3: 2}[step], to_next, to_previous)
    if step == 1:
        place_all(potentials, table, sems, slots)
    else:
        copy_slots(slots, held)
        add_slot(held, chain_slot(step - 1, s, child_drop, parent_drop), refs[4])
        place_all(potentials, table, sems, held)
    chosen_margin(table, axis, message)


def root_margins_kernel(child_drop, parent_drop, potentials, slots, first, second, third, margins, full, table, sems):
    me, s = lax.axis_index("clique"), lax.axis_index("subtree")
    load(potentials, table, sems)
    copy_slots(slots, full)

    @pl.when(me == 0)
    def _():
        for step, arrived in ((1, first), (2, second), (3, third)):
            add_slot(full, chain_slot(step, s, child_drop, parent_drop), arrived)

    place_all(potentials, table, sems, full)
    for k in range(4):
        MARGINS[k](table, slot_store(margins, k))


def child_margins_kernel(child_drop, potentials, slots, received, message, margins, table, held, sems):
    me, s = lax.axis_index("clique"), lax.axis_index("subtree")
    load(potentials, table, sems)
    copy_slots(slots, held)

    @pl.when(me != 0)
    def _():
        add_slot(held, child_drop[s, me], received, minus=message)

    place_all(potentials, table, sems, held)
    for k in range(4):
        MARGINS[k](table, slot_store(margins, k))


def final_kernel(child_drop, potentials, slots, received, message, out, table, held, sems, out_sems):
    me, s = lax.axis_index("clique"), lax.axis_index("subtree")
    load(potentials, table, sems)
    copy_slots(slots, held)
    top = received[0]
    for piece in range(1, PIECES):
        top = jnp.maximum(top, received[piece])
    top = jnp.max(top)
    total = jnp.zeros((8, 128), F32)
    for piece in range(PIECES):
        total = total + jnp.exp(received[piece] - top)
    log_total = top + jnp.log(jnp.broadcast_to(jnp.sum(total), (8, 128)))
    drop = child_drop[s, me]

    @pl.when(me != 0)
    def _():
        add_slot(held, drop, received, minus=message, shift=log_total)

    @pl.when(me == 0)
    def _():
        def body(piece, carry):
            held[piece, drop] = held[piece, drop] - log_total
            return carry

        lax.fori_loop(0, PIECES, body, 0)

    size = 1024 // CHUNKS

    def out_copy(chunk):
        part = pl.ds(pl.multiple_of(chunk * size, size), size)
        return pltpu.make_async_copy(table.at[part], out.at[part], out_sems.at[chunk])

    place_all(potentials, table, sems, held, after=lambda chunk: out_copy(chunk).start())
    for chunk in range(CHUNKS):
        out_copy(chunk).wait()


def enter(me):
    barrier = pltpu.get_barrier_semaphore()

    def body(d, carry):
        pl.semaphore_signal(barrier, inc=1, device_id={"clique": (me + d) % PIECES}, device_id_type=MESH)
        return carry

    lax.fori_loop(1, PIECES, body, 0)
    pl.semaphore_wait(barrier, PIECES - 1)


def send_pieces(me, source, target, sems):
    def body(d, carry):
        other = (me + d) % PIECES
        pltpu.make_async_remote_copy(
            src_ref=source.at[other],
            dst_ref=target.at[me],
            send_sem=sems.at[0],
            recv_sem=sems.at[1],
            device_id={"clique": other},
            device_id_type=MESH,
        ).start()
        return carry

    lax.fori_loop(1, PIECES, body, 0)


def all_but_one(me, source, target, sems):
    return pltpu.make_async_remote_copy(
        src_ref=source.at[pl.ds(0, PIECES - 1)],
        dst_ref=target.at[pl.ds(0, PIECES - 1)],
        send_sem=sems.at[0],
        recv_sem=sems.at[1],
        device_id={"clique": (me + 1) % PIECES},
        device_id_type=MESH,
    )


def gather_up(me, previous, last, message, arrived, sums, sems):
    enter(me)
    send_pieces(me, message, arrived, sems)
    arrived[me] = message[me]
    all_but_one(me, message, arrived, sems).wait_recv()
    sums[PIECES] = jnp.zeros((8, 128), F32)
    for c in range(1, PIECES):
        sums[c] = arrived[c] + sums[previous[c]]
    all_but_one(me, message, arrived, sems).wait_send()


def sums_kernel(previous, last, message, slots, arrived, sums, outgoing, incoming, sems, more_sems):
    me = lax.axis_index("clique")
    gather_up(me, previous, last, message, arrived, sums, sems)

    def body(p, carry):
        for k in range(4):
            outgoing[p, k] = sums[last[p * 4 + k]]
        return carry

    lax.fori_loop(0, PIECES, body, 0)
    send_pieces(me, outgoing, incoming, more_sems)
    incoming[me] = outgoing[me]
    all_but_one(me, outgoing, incoming, more_sems).wait()
    copy_slots(incoming, slots)


def root_sums_kernel(previous, last, message, old_slots, slots, arrived, sums, outgoing, incoming, sems, more_sems):
    me = lax.axis_index("clique")
    gather_up(me, previous, last, message, arrived, sums, sems)
    for k in range(4):
        outgoing[k] = sums[last[k]]

    @pl.when(me != 0)
    def _():
        copy = pltpu.make_async_remote_copy(
            src_ref=outgoing,
            dst_ref=incoming.at[me],
            send_sem=more_sems.at[0],
            recv_sem=more_sems.at[1],
            device_id={"clique": 0},
            device_id_type=MESH,
        )
        copy.start()
        copy_slots(old_slots, slots)
        copy.wait_send()

    @pl.when(me == 0)
    def _():
        for k in range(4):
            slots[0, k] = outgoing[k]
        pltpu.make_async_remote_copy(
            src_ref=incoming.at[pl.ds(1, PIECES - 1)],
            dst_ref=incoming.at[pl.ds(1, PIECES - 1)],
            send_sem=more_sems.at[0],
            recv_sem=more_sems.at[1],
            device_id={"clique": 1},
            device_id_type=MESH,
        ).wait_recv()

        def body(piece, carry):
            for k in range(4):
                slots[piece, k] = incoming[piece, k]
            return carry

        lax.fori_loop(1, PIECES, body, 0)


def send_received(me, outgoing, received, incoming, sems):
    send_pieces(me, outgoing, incoming, sems)
    incoming[me] = outgoing[me]
    all_but_one(me, outgoing, incoming, sems).wait()

    def body(piece, carry):
        received[piece] = incoming[piece]
        return carry

    lax.fori_loop(0, PIECES, body, 0)


def root_spread_kernel(parent_drop, margins, received, arrived, outgoing, incoming, sems, more_sems):
    me, s = lax.axis_index("clique"), lax.axis_index("subtree")
    enter(me)

    @pl.when(me == 0)
    def _():
        def body(other, carry):
            pltpu.make_async_remote_copy(
                src_ref=margins.at[other],
                dst_ref=arrived,
                send_sem=sems.at[0],
                recv_sem=sems.at[1],
                device_id={"clique": other},
                device_id_type=MESH,
            ).start()
            return carry

        lax.fori_loop(1, PIECES, body, 0)
        for k in range(4):
            arrived[k] = margins[0, k]

    @pl.when(me != 0)
    def _():
        pltpu.make_async_remote_copy(
            src_ref=arrived,
            dst_ref=arrived,
            send_sem=sems.at[0],
            recv_sem=sems.at[1],
            device_id={"clique": 0},
            device_id_type=MESH,
        ).wait_recv()

    for c in range(PIECES):
        outgoing[c] = arrived[parent_drop[s, c]]
    send_received(me, outgoing, received, incoming, more_sems)

    @pl.when(me == 0)
    def _():
        pltpu.make_async_remote_copy(
            src_ref=margins.at[pl.ds(1, PIECES - 1)],
            dst_ref=margins.at[pl.ds(1, PIECES - 1)],
            send_sem=sems.at[0],
            recv_sem=sems.at[1],
            device_id={"clique": 1},
            device_id_type=MESH,
        ).wait_send()


def spread_kernel(parent, parent_drop, margins, received, arrived, outgoing, incoming, sems, more_sems):
    me, s = lax.axis_index("clique"), lax.axis_index("subtree")
    enter(me)
    send_pieces(me, margins, arrived, sems)
    arrived[me] = margins[me]
    all_but_one(me, margins, arrived, sems).wait_recv()
    for c in range(PIECES):
        outgoing[c] = arrived[parent[0, c], parent_drop[s, c]]
    send_received(me, outgoing, received, incoming, more_sems)
    all_but_one(me, margins, arrived, sems).wait_send()


MESSAGE = jax.ShapeDtypeStruct((PIECES, 8, 128), F32)
SLOTS = jax.ShapeDtypeStruct((PIECES, 4, 8, 128), F32)
TABLE = jax.ShapeDtypeStruct((1024, 1024), F32)
ANY_SPEC = pl.BlockSpec(memory_space=pl.ANY)
S_SPEC = pl.BlockSpec(memory_space=SMEM)
V_SPEC = pl.BlockSpec(memory_space=VMEM)
HELD_MESSAGE = VMEM((PIECES, 8, 128), F32)
HELD_SUMS = VMEM((PIECES + 1, 8, 128), F32)
HELD_SLOTS = VMEM((PIECES, 4, 8, 128), F32)
HELD_PIECE = VMEM((4, 8, 128), F32)
HELD_TABLE = VMEM((1024, 1024), F32)
LOAD_SEMS = pltpu.SemaphoreType.DMA((CHUNKS,))
PAIR_SEMS = pltpu.SemaphoreType.DMA((2,))


def call(kernel, name, ins, outs, out_specs, scratch, collective=None):
    more = {} if collective is None else dict(collective_id=collective, has_side_effects=True)
    return pl.pallas_call(
        kernel,
        name=name,
        in_specs=ins,
        out_shape=outs,
        out_specs=out_specs,
        scratch_shapes=scratch,
        compiler_params=pltpu.CompilerParams(vmem_limit_bytes=40 * 2**20, **more),
    )


def per_device(potentials, parent, child_drop, parent_drop):
    table = potentials.reshape(1024, 1024)
    compute = [HELD_TABLE]
    message, previous, last = call(
        first_kernel,
        "first",
        [S_SPEC] * 3 + [ANY_SPEC],
        (MESSAGE, jax.ShapeDtypeStruct((PIECES,), jnp.int32), jax.ShapeDtypeStruct((4 * PIECES,), jnp.int32)),
        (V_SPEC, S_SPEC, S_SPEC),
        [HELD_TABLE, LOAD_SEMS],
    )(parent, child_drop, parent_drop, table)
    slots = call(
        sums_kernel,
        "sums",
        [S_SPEC] * 2 + [V_SPEC],
        SLOTS,
        V_SPEC,
        [HELD_MESSAGE, HELD_SUMS, HELD_SLOTS, HELD_SLOTS, PAIR_SEMS, PAIR_SEMS],
        collective=0,
    )(previous, last, message)
    message = call(
        up_kernel, "up", [S_SPEC, ANY_SPEC, V_SPEC], MESSAGE, V_SPEC, [HELD_TABLE, LOAD_SEMS]
    )(child_drop, table, slots)
    slots = call(
        root_sums_kernel,
        "root_sums",
        [S_SPEC] * 2 + [V_SPEC] * 2,
        SLOTS,
        V_SPEC,
        [HELD_MESSAGE, HELD_SUMS, HELD_PIECE, HELD_SLOTS, PAIR_SEMS, PAIR_SEMS],
        collective=1,
    )(previous, last, message, slots)
    arrived = []
    for step, pairs in ((1, ((3, 2), (0, 1))), (2, ((2, 1), (1, 2))), (3, ((1, 0), (2, 3)))):
        sent = call(
            functools.partial(chain_kernel, step),
            f"chain_{step}",
            [S_SPEC] * 2 + [ANY_SPEC] + [V_SPEC] * (1 if step == 1 else 2),
            MESSAGE,
            V_SPEC,
            [HELD_TABLE, HELD_SLOTS, LOAD_SEMS],
        )(child_drop, parent_drop, table, slots, *arrived[step - 2 : step - 1])
        arrived.append(lax.ppermute(sent, ("clique", "subtree"), pairs))
    margins, slots = call(
        root_margins_kernel,
        "root_margins",
        [S_SPEC] * 2 + [ANY_SPEC] + [V_SPEC] * 4,
        (SLOTS, SLOTS),
        (V_SPEC, V_SPEC),
        [HELD_TABLE, LOAD_SEMS],
    )(child_drop, parent_drop, table, slots, *arrived)
    received = call(
        root_spread_kernel,
        "root_spread",
        [S_SPEC, V_SPEC],
        MESSAGE,
        V_SPEC,
        [HELD_PIECE, HELD_MESSAGE, HELD_MESSAGE, PAIR_SEMS, PAIR_SEMS],
        collective=2,
    )(parent_drop, margins)
    margins = call(
        child_margins_kernel,
        "child_margins",
        [S_SPEC, ANY_SPEC] + [V_SPEC] * 3,
        SLOTS,
        V_SPEC,
        [HELD_TABLE, HELD_SLOTS, LOAD_SEMS],
    )(child_drop, table, slots, received, message)
    received = call(
        spread_kernel,
        "spread",
        [S_SPEC, S_SPEC, V_SPEC],
        MESSAGE,
        V_SPEC,
        [HELD_SLOTS, HELD_MESSAGE, HELD_MESSAGE, PAIR_SEMS, PAIR_SEMS],
        collective=3,
    )(parent, parent_drop, margins)
    out = call(
        final_kernel,
        "final",
        [S_SPEC, ANY_SPEC] + [V_SPEC] * 3,
        TABLE,
        ANY_SPEC,
        [HELD_TABLE, HELD_SLOTS, LOAD_SEMS, LOAD_SEMS],
    )(child_drop, table, slots, received, message)
    return out.reshape(1, 1, 1024, 1024)


def solution(mesh):
    specs = (P("subtree", "clique", None, None), P("subtree", None), P(), P())
    return jax.shard_map(
        per_device,
        mesh=mesh,
        in_specs=specs,
        out_specs=P("subtree", "clique", None, None),
        check_vma=False,
    )
```

time: 647 us -> 316 us (0.49); the launches traced: 636 us -> 316 us
  Pallas kernels: 0 us -> 310 us
  waiting for transfers between devices: 243 us -> 0.01 us
  local copies, waits for them, and re-layouts: 143 us -> 4.22 us
  other arithmetic: 108 us -> 0 us
  matrix products: 82.6 us -> 0 us
  loops' own time: 26.5 us -> 0 us
  between operations: 17.8 us -> 0.17 us
  starting transfers between devices: 14.8 us -> 2.01 us
    pallas_call x0 -> x12, Pallas kernels: none -> 310 us  [the longest x3 51.2 us: per_device(): call(functools.partial(chain_kernel, step), f'chain_{step}', [S_SPEC] * 2...]
    all_gather x4 -> x0, waiting for transfers between devices: 224 us -> none  [the longest x2 129 us: per_device(): lax.all_gather(margins(belief), 'clique', axis=0, tiled=True)]
    dot_general x15 -> x0, matrix products: 82.6 us -> none  [the longest x11 57 us: spread_slots(): jnp.einsum('nab,bc->nac', back_slots, spread_table, precision=lax.Precisi...]
    unnamed x44 -> x14, local copies, waits for them, and re-layouts: 58.3 us -> 4.22 us
    reduce_sum x19 -> x0, other arithmetic: 46.1 us -> none  [the longest x18 43.7 us: log_sum(): jnp.sum(jnp.exp(stacked - top), axis=axis)]
    add x38 -> x0, local copies, waits for them, and re-layouts: 40.2 us -> none
    reduce_max x16 -> x0, other arithmetic: 40.1 us -> none  [log_sum(): top = jnp.max(stacked, axis=axis, keepdims=True)]
    another operation x10 -> x0, loops' own time: 26.5 us -> none  [one_clique(): lax.switch(pair[1], [margin_first, margin_second, margin_third, margin_fo...]
  transfers between devices with their start and end apart: 10 -> 3, of which waited for: 9 -> 0; matrix products, arithmetic and copies ran while one was open for 3% -> 0% of each run, Pallas kernels for 0% -> 0%
where the time goes in v1:
time: 316 us
  Pallas kernels  310 us (98%)
  local copies, waits for them, and re-layouts  4.22 us (1%)
    pallas_call x3, Pallas kernels, per_device(): call(functools.partial(chain_kernel, step), f'chain_{step}', [S_SPEC] * 2...  51.2 us
    pallas_call x1, Pallas kernels, per_device(): call(child_margins_kernel, 'child_margins', [S_SPEC, ANY_SPEC] + [V_SPEC]...  49.7 us
    pallas_call x1, Pallas kernels, per_device(): call(root_margins_kernel, 'root_margins', [S_SPEC] * 2 + [ANY_SPEC] + [V_...  49.6 us
    pallas_call x1, Pallas kernels, per_device(): call(sums_kernel, 'sums', [S_SPEC] * 2 + [V_SPEC], SLOTS, V_SPEC, [HELD_M...  41.8 us
    pallas_call x1, Pallas kernels, per_device(): call(root_spread_kernel, 'root_spread', [S_SPEC, V_SPEC], MESSAGE, V_SPEC...  32 us
    pallas_call x1, Pallas kernels, per_device(): call(root_sums_kernel, 'root_sums', [S_SPEC] * 2 + [V_SPEC] * 2, SLOTS, V...  29.1 us
    pallas_call x1, Pallas kernels, per_device(): call(spread_kernel, 'spread', [S_SPEC, S_SPEC, V_SPEC], MESSAGE, V_SPEC,...  18.4 us
    pallas_call x1, Pallas kernels, per_device(): call(up_kernel, 'up', [S_SPEC, ANY_SPEC, V_SPEC], MESSAGE, V_SPEC, [HELD_...  16.8 us
  transfers between devices with their start and end apart: 3, of which 0 were waited for; matrix products, arithmetic and copies ran while one was open for 0% of the time, Pallas kernels for 0%

profile of v1, /device:TPU:1, one launch (start us, length us, event | category | flops | bytes accessed | tf_op | source)
XLA Modules:
  0.0 316.1 jit_solution(16251127562119400146)
XLA Ops:
  0.0 2.2 copy-done
  2.2 0.7 copy-done.2
  2.9 0.7 copy-done.4
  3.6 0.7 copy-done.6
  4.2 13.0 %first.1 = (f32[32,8,128]{2,1,0:T(8,128)S(1)}, s32[32]{0:T(128)S(1)}, s32[128]{0:T(128)S(1)}) custom-call(s32[1,32]{1,0:T(1,128)S(1)} %copy-done.6, s32[4,32]{1,0:T(4,128)S(1)} %copy-done.2, s32[4,32]{1,0:T(4,128)S(1)} %copy-done.4, f32[1024,1024]{1,0:T(8,128)S(1)} %bitcast.2), custom_call_target="tpu_custom_call" | custom-call | tf_op jit(solution)/shard_map/first/pallas_call | solution.py:576
  17.2 41.8 %sums.1.slots.old_slots = f32[32,4,8,128]{3,2,1,0:T(8,128)S(1)} custom-call(s32[32]{0:T(128)S(1)} %get-tuple-element.10.previous, s32[128]{0:T(128)S(1)} %get-tuple-element.11.last, f32[32,8,128]{2,1,0:T(8,128)S(1)} %get-tuple-element.12.message), custom_call_target="tpu_custom_call" | custom-call | tf_op jit(solution)/shard_map/sums/pallas_call | solution.py:584
  59.0 0.0 copy-done.1
  59.0 16.8 %up.1.message = f32[32,8,128]{2,1,0:T(8,128)S(1)} custom-call(s32[4,32]{1,0:T(4,128)S(1)} %copy-done.3, f32[1024,1024]{1,0:T(8,128)S(1)} %bitcast.3, f32[32,4,8,128]{3,2,1,0:T(8,128)S(1)} %sums.1.slots.old_slots), custom_call_target="tpu_custom_call" | custom-call | tf_op jit(solution)/shard_map/up/pallas_call | solution.py:593
  75.8 0.0 copy-start.5
  75.8 29.1 %root_sums.1.refs_3_.slots = f32[32,4,8,128]{3,2,1,0:T(8,128)S(1)} custom-call(s32[32]{0:T(128)S(1)} %get-tuple-element.10.previous, s32[128]{0:T(128)S(1)} %get-tuple-element.11.last, f32[32,8,128]{2,1,0:T(8,128)S(1)} %up.1.message, f32[32,4,8,128]{3,2,1,0:T(8,128)S(1)} %sums.1.slots.old_slots), custom_call_target="tpu_custom_call" | custom-call | tf_op jit(solution)/shard_map/root_sums/pallas_call | solution.py:596
  104.9 16.8 %chain_1.1 = f32[32,8,128]{2,1,0:T(8,128)S(1)} custom-call(s32[4,32]{1,0:T(4,128)S(1)} %copy-done.3, s32[4,32]{1,0:T(4,128)S(1)} %copy-done.4, f32[1024,1024]{1,0:T(8,128)S(1)} %bitcast.4, f32[32,4,8,128]{3,2,1,0:T(8,128)S(1)} %root_sums.1.refs_3_.slots), custom_call_target="tpu_custom_call" | custom-call | tf_op jit(solution)/shard_map/chain_1/pallas_call | solution.py:607
  121.7 0.7 collective-permute-start
  122.4 0.0 collective-permute-done.refs_4_.first
  122.4 17.2 %chain_2.1 = f32[32,8,128]{2,1,0:T(8,128)S(1)} custom-call(s32[4,32]{1,0:T(4,128)S(1)} %copy-done.3, s32[4,32]{1,0:T(4,128)S(1)} %copy-done.5, f32[1024,1024]{1,0:T(8,128)S(1)} %bitcast.5, f32[32,4,8,128]{3,2,1,0:T(8,128)S(1)} %root_sums.1.refs_3_.slots, f32[32,8,128]{2,1,0:T(8,128)S(1)} %collective-permute-done.refs_4_.first), custom_call_target="tpu_custom_call" | custom-call | tf_op jit(solution)/shard_map/chain_2/pallas_call | solution.py:607
  139.6 0.7 collective-permute-start.1
  140.3 0.0 collective-permute-done.1.refs_4_.second
  140.3 17.2 %chain_3.1 = f32[32,8,128]{2,1,0:T(8,128)S(1)} custom-call(s32[4,32]{1,0:T(4,128)S(1)} %copy-done.3, s32[4,32]{1,0:T(4,128)S(1)} %copy-done.5, f32[1024,1024]{1,0:T(8,128)S(1)} %bitcast.6, f32[32,4,8,128]{3,2,1,0:T(8,128)S(1)} %root_sums.1.refs_3_.slots, f32[32,8,128]{2,1,0:T(8,128)S(1)} %collective-permute-done.1.refs_4_.second), custom_call_target="tpu_custom_call" | custom-call | tf_op jit(solution)/shard_map/chain_3/pallas_call | solution.py:607
  157.5 0.7 collective-permute-start.2
  158.2 0.0 collective-permute-done.2.third
  158.2 49.6 %root_margins.1 = (f32[32,4,8,128]{3,2,1,0:T(8,128)S(1)}, f32[32,4,8,128]{3,2,1,0:T(8,128)S(1)}) custom-call(s32[4,32]{1,0:T(4,128)S(1)} %copy-done.3, s32[4,32]{1,0:T(4,128)S(1)} %copy-done.5, f32[1024,1024]{1,0:T(8,128)S(1)} %bitcast.7, f32[32,4,8,128]{3,2,1,0:T(8,128)S(1)} %root_sums.1.refs_3_.slots, ...), custom_call_target="tpu_custom_call" | custom-call | tf_op jit(solution)/shard_map/root_margins/pallas_call | solution.py:616
  207.8 32.0 %root_spread.1.received = f32[32,8,128]{2,1,0:T(8,128)S(1)} custom-call(s32[4,32]{1,0:T(4,128)S(1)} %copy-done.5, f32[32,4,8,128]{3,2,1,0:T(8,128)S(1)} %get-tuple-element.14.margins), custom_call_target="tpu_custom_call" | custom-call | tf_op jit(solution)/shard_map/root_spread/pallas_call | solution.py:624
  239.8 49.7 %child_margins.1.margins = f32[32,4,8,128]{3,2,1,0:T(8,128)S(1)} custom-call(s32[4,32]{1,0:T(4,128)S(1)} %copy-done.3, f32[1024,1024]{1,0:T(8,128)S(1)} %bitcast.8, f32[32,4,8,128]{3,2,1,0:T(8,128)S(1)} %get-tuple-element.13.slots, f32[32,8,128]{2,1,0:T(8,128)S(1)} %root_spread.1.received, f32[32,8,128]{2,1,0:T(8,128)S(1)} %up.1.message), custom_call_target="tpu_custom_call" | custom-call | tf_op jit(solution)/shard_map/child_margins/pallas_call | solution.py:633
  289.5 18.4 %spread.1.received = f32[32,8,128]{2,1,0:T(8,128)S(1)} custom-call(s32[1,32]{1,0:T(1,128)S(1)} %copy-done.6, s32[4,32]{1,0:T(4,128)S(1)} %copy-done.5, f32[32,4,8,128]{3,2,1,0:T(8,128)S(1)} %child_margins.1.margins), custom_call_target="tpu_custom_call" | custom-call | tf_op jit(solution)/shard_map/spread/pallas_call | solution.py:641
  308.0 8.1 %final.1 = f32[1024,1024]{1,0:T(8,128)} custom-call(s32[4,32]{1,0:T(4,128)S(1)} %copy-done.3, f32[1024,1024]{1,0:T(8,128)S(1)} %bitcast.9, f32[32,4,8,128]{3,2,1,0:T(8,128)S(1)} %get-tuple-element.13.slots, f32[32,8,128]{2,1,0:T(8,128)S(1)} %spread.1.received, f32[32,8,128]{2,1,0:T(8,128)S(1)} %up.1.message), custom_call_target="tpu_custom_call" | custom-call | tf_op jit(solution)/shard_map/final/pallas_call | solution.py:650
  (8 shorter events, 0.0 us)
Async XLA Ops:
  0.0 2.2 copy-start
  2.2 0.7 copy-start.2
  2.9 0.7 copy-start.4
  3.6 0.7 copy-start.6
  4.2 54.8 %copy-start.1 = (f32[1,1,1024,1024]{3,2,1,0:T(8,128)S(1)}, f32[1,1,1024,1024]{3,2,1,0:T(8,128)}, u32[]{:S(2)}) copy-start(f32[1,1,1024,1024]{3,2,1,0:T(8,128)} %param.4) | copy-start | bytes 12582916
  4.2 54.8 %copy-start.3 = (s32[4,32]{1,0:T(4,128)S(1)}, s32[4,32]{1,0:T(4,128)}, u32[]{:S(2)}) copy-start(s32[4,32]{1,0:T(4,128)} %child_drop.9) | copy-start | bytes 1540
  75.8 46.6 %copy-start.5 = (s32[4,32]{1,0:T(4,128)S(1)}, s32[4,32]{1,0:T(4,128)}, u32[]{:S(2)}) copy-start(s32[4,32]{1,0:T(4,128)} %parent_drop.7) | copy-start | bytes 1540
  121.7 0.7 collective-permute-start
  139.6 0.7 collective-permute-start.1
  157.5 0.7 collective-permute-start.2

commit v2 on v1

v2 whole, which is shorter than its diff:
```python
import functools

import jax
import jax.numpy as jnp
from jax import lax
from jax.experimental import pallas as pl
from jax.experimental.pallas import tpu as pltpu
from jax.sharding import PartitionSpec as P

PIECES = 32
CHUNKS = 8
MESH = pl.DeviceIdType.MESH
F32 = jnp.float32
VMEM = pltpu.VMEM
SMEM = pltpu.SMEM


def lanes():
    return lax.broadcasted_iota(jnp.int32, (8, 128), 1)


def rows():
    return lax.broadcasted_iota(jnp.int32, (8, 128), 0)


def take(vec, index):
    return jnp.take_along_axis(vec, index, axis=1, mode="promise_in_bounds")


def tree(parts, op):
    parts = list(parts)
    while len(parts) > 1:
        parts = [op(*parts[n : n + 2]) if n + 1 < len(parts) else parts[n] for n in range(0, len(parts), 2)]
    return parts[0]


def tile(table, a0, i, t):
    return table[pl.ds(pl.multiple_of(a0 * 32 + 8 * i, 8), 8), 128 * t : 128 * (t + 1)]


def place(source, target, terms, after=None):
    lane, row = lanes(), rows()
    spread_third = (row % 4) * 32 + lane % 32
    spread_fourth = [(row % 4) * 32 + lane // 32 + 4 * t for t in range(8)]

    def body(part, carry):
        for s in range(8):
            a0 = part * 8 + s

            def slot_row(k, j):
                return terms[k][1](part * 8 + j, s)

            second = [slot_row(1, t) for t in range(8)] if 1 in terms else None
            for i in range(4):
                both = {
                    k: jnp.where(row < 4, slot_row(k, 2 * i), slot_row(k, 2 * i + 1))
                    for k in (2, 3)
                    if k in terms
                }
                third = take(both[2], spread_third) if 2 in terms else None
                for t in range(8):
                    adds = [tile(source, a0, i, t)]
                    if 0 in terms:
                        adds.append(terms[0][0](i * 8 + t))
                    if 1 in terms:
                        adds.append(jnp.broadcast_to(second[t], (8, 128)))
                    if 2 in terms:
                        adds.append(third)
                    if 3 in terms:
                        adds.append(take(both[3], spread_fourth[t]))
                    where = pl.ds(pl.multiple_of(a0 * 32 + 8 * i, 8), 8)
                    target[where, 128 * t : 128 * (t + 1)] = tree(adds, jnp.add)
        if after is not None:
            after(part)
        return carry

    lax.fori_loop(0, 4, body, 0)


def place_slots(source, target, slots, after=None):
    def readers(k):
        return lambda piece: slots[piece, k], lambda piece, s: slots[piece, k, pl.ds(s, 1), :]

    place(source, target, {k: readers(k) for k in range(4)}, after)


def place_message(source, target, message, axis, after=None):
    for k in range(4):

        @pl.when(axis == k)
        def _(k=k):
            readers = (lambda piece: message[piece], lambda piece, s: message[piece, pl.ds(s, 1), :])
            place(source, target, {k: readers}, after)


def pick(parts):
    group = lanes() // 32
    return jnp.where(
        group == 0, parts[0], jnp.where(group == 1, parts[1], jnp.where(group == 2, parts[2], parts[3]))
    )


def margin_0(table, put, work):
    def body(i, carry):
        for t in range(8):
            parts = [tile(table, a0, i, t) for a0 in range(32)]
            top = tree(parts, jnp.maximum)
            total = tree([jnp.exp(part - top) for part in parts], jnp.add)
            put(i * 8 + t, 1, None, top + jnp.log(total))
        return carry

    lax.fori_loop(0, 4, body, 0)


def over_rows(vec, op):
    for shift in (4, 2, 1):
        vec = op(vec, pltpu.roll(vec, shift, 0))
    return vec


def margin_1(table, put, work):
    def body(a0, carry):
        for t in range(8):
            parts = [tile(table, a0, i, t) for i in range(4)]
            top = over_rows(tree(parts, jnp.maximum), jnp.maximum)
            total = over_rows(tree([jnp.exp(part - top) for part in parts], jnp.add), jnp.add)
            put((a0 // 8) * 8 + t, 1, a0 % 8, (top + jnp.log(total))[0:1])
        return carry

    lax.fori_loop(0, 32, body, 0)


def margin_2(table, put, work):
    totals, tops = work[0], work[1]

    def largest(a0, carry):
        for i in range(4):
            at = pl.ds(pl.multiple_of((a0 * 4 + i) * 8, 8), 8)
            totals[at, :] = tree([tile(table, a0, i, t) for t in range(8)], jnp.maximum)
        return carry

    lax.fori_loop(0, 32, largest, 0, unroll=4)

    def groups(n, carry):
        ats = [pl.ds(pl.multiple_of((n * 32 + m) * 8, 8), 8) for m in range(32)]
        parts = [totals[at, :] for at in ats]
        for shift in (64, 32):
            moved = [pltpu.roll(part, shift, 1) for part in parts]
            parts = [jnp.maximum(part, other) for part, other in zip(parts, moved)]
        for at, part in zip(ats, parts):
            tops[at, :] = part
        return carry

    lax.fori_loop(0, 4, groups, 0)

    def sums(a0, carry):
        for i in range(4):
            at = pl.ds(pl.multiple_of((a0 * 4 + i) * 8, 8), 8)
            top = tops[at, :]
            totals[at, :] = tree([jnp.exp(tile(table, a0, i, t) - top) for t in range(8)], jnp.add)
        return carry

    lax.fori_loop(0, 32, sums, 0, unroll=2)

    def pack(part, carry):
        packed = []
        for s in range(8):
            start = (part * 8 + s) * 32
            total = [totals[pl.ds(start + q, 8, stride=4), :] for q in range(4)]
            top = pick([tops[pl.ds(start + q, 8, stride=4), :] for q in range(4)])
            turned = [pick([total[(g + r) % 4] for g in range(4)]) for r in range(4)]
            packed.append((top, [turned[0]] + [pltpu.roll(turned[r], 32 * r, 1) for r in range(1, 4)]))
        for s, (top, turned) in enumerate(packed):
            put(part * 8, 8, s, top + jnp.log((turned[0] + turned[1]) + (turned[2] + turned[3])))
        return carry

    lax.fori_loop(0, 4, pack, 0)


def margin_3(table, put, work):
    flat, across = work[0], work[2]

    def body(block, carry):
        for t in range(8):
            turned = table[pl.ds(pl.multiple_of(block * 128, 128), 128), 128 * t : 128 * (t + 1)].T
            for g in range(4):
                parts = [turned[32 * g + 8 * m : 32 * g + 8 * (m + 1)] for m in range(4)]
                top = over_rows(tree(parts, jnp.maximum), jnp.maximum)
                total = over_rows(tree([jnp.exp(part - top) for part in parts], jnp.add), jnp.add)
                across[block, 4 * t + g : 4 * t + g + 1, :] = (top + jnp.log(total))[0:1]
        return carry

    lax.fori_loop(0, 8, body, 0, unroll=2)
    for block in range(8):
        part = across[block]
        flat[128 * block : 128 * (block + 1), :] = jnp.concatenate([part] * 4, axis=0).T
    for a0 in range(32):
        put((a0 // 8) * 8, 8, a0 % 8, pick([flat[pl.ds(a0 * 32 + q, 8, stride=4), :] for q in range(4)]))


MARGINS = (margin_0, margin_1, margin_2, margin_3)


def message_put(message):
    def put(piece, count, row, value):
        if row is None:
            message[piece] = value
        elif count == 1:
            message[piece, pl.ds(row, 1), :] = value
        else:
            message[pl.ds(piece, count), row, :] = value

    return put


def slot_put(slots, k):
    def put(piece, count, row, value):
        if row is None:
            slots[piece, k] = value
        elif count == 1:
            slots[piece, k, pl.ds(row, 1), :] = value
        else:
            slots[pl.ds(piece, count), k, row, :] = value

    return put


def chosen_margin(table, axis, message, work):
    for k in range(4):

        @pl.when(axis == k)
        def _(k=k):
            MARGINS[k](table, message_put(message), work)


def copy_slots(source, target):
    def body(piece, carry):
        for k in range(4):
            target[piece, k] = source[piece, k]
        return carry

    lax.fori_loop(0, PIECES, body, 0)


PREVIOUS, LAST, SOURCE, OWN_DROP, CHAIN_AXIS, CHAIN_SLOT, INFO = 0, 32, 160, 192, 192, 196, 256


def first_kernel(trees_in, potentials, message, info, table, trees, *rest):
    work, load_sems, sems = rest[:3], rest[3], rest[4]
    me, s = lax.axis_index("clique"), lax.axis_index("subtree")
    size = 1024 // CHUNKS
    loads = [
        pltpu.make_async_copy(
            potentials.at[pl.ds(size * n, size)], table.at[pl.ds(size * n, size)], load_sems.at[n]
        )
        for n in range(CHUNKS)
    ]
    small = pltpu.make_async_copy(trees_in, trees, sems)
    small.start()
    for copy in loads:
        copy.start()
    for n in range(128):
        info[LAST + n] = PIECES
    small.wait()
    info[PREVIOUS] = PIECES
    info[SOURCE] = trees[4 + s, 0]

    def link(c, carry):
        target = trees[8, c] * 4 + trees[4 + s, c]
        info[SOURCE + c] = target
        info[PREVIOUS + c] = info[LAST + target]
        info[LAST + target] = c
        return carry

    lax.fori_loop(1, PIECES, link, 0)
    own = trees[s, me]
    info[OWN_DROP] = own
    to_next = trees[4 + jnp.minimum(s + 1, 3), 0]
    to_previous = trees[s, 0]
    for step, sender, receiver in ((1, 0, 2), (2, 1, 1), (3, 2, 0)):
        info[CHAIN_AXIS + step] = jnp.where(s == sender, to_next, to_previous)
        info[CHAIN_SLOT + step] = jnp.where(s == receiver, to_next, to_previous)
    for copy in loads:
        copy.wait()
    chosen_margin(table, own, message, work)


def up_kernel(info, table, slots, message, placed, *work):
    place_slots(table, placed, slots)
    chosen_margin(placed, info[OWN_DROP], message, work)


def chain_first_kernel(info, table, slots, message, placed, *work):
    place_slots(table, placed, slots)
    chosen_margin(placed, info[CHAIN_AXIS + 1], message, work)


def chain_kernel(step, info, table, arrived, message, placed, *work):
    place_message(table, placed, arrived, info[CHAIN_SLOT + step - 1])
    chosen_margin(placed, info[CHAIN_AXIS + step], message, work)


def all_margins(table, margins, work):
    for k in range(4):
        MARGINS[k](table, slot_put(margins, k), work)


def root_margins_kernel(info, table, first, third, margins, belief, held, *work):
    s = lax.axis_index("subtree")
    inner = (s == 1) | (s == 2)

    def body(piece, carry):
        held[piece] = jnp.where(inner, first[piece], third[piece])
        return carry

    lax.fori_loop(0, PIECES, body, 0)
    place_message(table, belief, held, jnp.where(inner, info[CHAIN_SLOT + 1], info[CHAIN_SLOT + 3]))
    all_margins(belief, margins, work)


def child_margins_kernel(info, table, received, message, margins, belief, held, *work):
    below = lax.axis_index("clique") != 0

    def body(piece, carry):
        held[piece] = jnp.where(below, received[piece] - message[piece], 0.0)
        return carry

    lax.fori_loop(0, PIECES, body, 0)
    place_message(table, belief, held, info[OWN_DROP])
    all_margins(belief, margins, work)


def final_kernel(info, table, received, message, out, belief, held, sems):
    below = lax.axis_index("clique") != 0
    top = jnp.max(tree([received[piece] for piece in range(PIECES)], jnp.maximum))
    total = tree([jnp.exp(received[piece] - top) for piece in range(PIECES)], jnp.add)
    log_total = top + jnp.log(jnp.broadcast_to(jnp.sum(total), (8, 128)))
    for piece in range(PIECES):
        held[piece] = jnp.where(below, received[piece] - message[piece], 0.0) - log_total

    def out_copy(part):
        at = pl.ds(pl.multiple_of(part * 256, 256), 256)
        return pltpu.make_async_copy(belief.at[at], out.at[at], sems.at[part])

    place_message(table, belief, held, info[OWN_DROP], after=lambda part: out_copy(part).start())
    for part in range(4):
        out_copy(part).wait()


def enter(me):
    barrier = pltpu.get_barrier_semaphore()

    def body(d, carry):
        pl.semaphore_signal(barrier, inc=1, device_id={"clique": (me + d) % PIECES}, device_id_type=MESH)
        return carry

    lax.fori_loop(1, PIECES, body, 0)
    pl.semaphore_wait(barrier, PIECES - 1)


def send_pieces(me, source, target, sems):
    def body(d, carry):
        other = (me + d) % PIECES
        pltpu.make_async_remote_copy(
            src_ref=source.at[other],
            dst_ref=target.at[me],
            send_sem=sems.at[0],
            recv_sem=sems.at[1],
            device_id={"clique": other},
            device_id_type=MESH,
        ).start()
        return carry

    lax.fori_loop(1, PIECES, body, 0)


def all_but_one(me, source, target, sems):
    return pltpu.make_async_remote_copy(
        src_ref=source.at[pl.ds(0, PIECES - 1)],
        dst_ref=target.at[pl.ds(0, PIECES - 1)],
        send_sem=sems.at[0],
        recv_sem=sems.at[1],
        device_id={"clique": (me + 1) % PIECES},
        device_id_type=MESH,
    )


def gather_up(me, info, message, arrived, sums, sems):
    enter(me)
    send_pieces(me, message, arrived, sems)
    arrived[me] = message[me]
    all_but_one(me, message, arrived, sems).wait_recv()
    sums[PIECES] = jnp.zeros((8, 128), F32)
    for c in range(1, PIECES):
        sums[c] = arrived[c] + sums[info[PREVIOUS + c]]
    all_but_one(me, message, arrived, sems).wait_send()


def sums_kernel(info, message, slots, arrived, sums, outgoing, incoming, sems, more_sems):
    me = lax.axis_index("clique")
    gather_up(me, info, message, arrived, sums, sems)

    def body(p, carry):
        for k in range(4):
            outgoing[p, k] = sums[info[LAST + p * 4 + k]]
        return carry

    lax.fori_loop(0, PIECES, body, 0)
    send_pieces(me, outgoing, incoming, more_sems)
    incoming[me] = outgoing[me]
    all_but_one(me, outgoing, incoming, more_sems).wait()
    copy_slots(incoming, slots)


def root_sums_kernel(info, message, old_slots, slots, arrived, sums, outgoing, incoming, sems, more_sems):
    me = lax.axis_index("clique")
    gather_up(me, info, message, arrived, sums, sems)
    for k in range(4):
        outgoing[k] = sums[info[LAST + k]]

    @pl.when(me != 0)
    def _():
        copy = pltpu.make_async_remote_copy(
            src_ref=outgoing,
            dst_ref=incoming.at[me],
            send_sem=more_sems.at[0],
            recv_sem=more_sems.at[1],
            device_id={"clique": 0},
            device_id_type=MESH,
        )
        copy.start()
        copy_slots(old_slots, slots)
        copy.wait_send()

    @pl.when(me == 0)
    def _():
        for k in range(4):
            slots[0, k] = outgoing[k]
        pltpu.make_async_remote_copy(
            src_ref=incoming.at[pl.ds(1, PIECES - 1)],
            dst_ref=incoming.at[pl.ds(1, PIECES - 1)],
            send_sem=more_sems.at[0],
            recv_sem=more_sems.at[1],
            device_id={"clique": 1},
            device_id_type=MESH,
        ).wait_recv()

        def body(piece, carry):
            for k in range(4):
                slots[piece, k] = incoming[piece, k]
            return carry

        lax.fori_loop(1, PIECES, body, 0)


def send_received(me, outgoing, received, incoming, sems):
    send_pieces(me, outgoing, incoming, sems)
    incoming[me] = outgoing[me]
    all_but_one(me, outgoing, incoming, sems).wait()

    def body(piece, carry):
        received[piece] = incoming[piece]
        return carry

    lax.fori_loop(0, PIECES, body, 0)


def root_spread_kernel(info, margins, received, arrived, outgoing, incoming, sems, more_sems):
    me = lax.axis_index("clique")
    enter(me)

    @pl.when(me == 0)
    def _():
        def body(other, carry):
            pltpu.make_async_remote_copy(
                src_ref=margins.at[other],
                dst_ref=arrived,
                send_sem=sems.at[0],
                recv_sem=sems.at[1],
                device_id={"clique": other},
                device_id_type=MESH,
            ).start()
            return carry

        lax.fori_loop(1, PIECES, body, 0)
        for k in range(4):
            arrived[k] = margins[0, k]

    @pl.when(me != 0)
    def _():
        pltpu.make_async_remote_copy(
            src_ref=arrived,
            dst_ref=arrived,
            send_sem=sems.at[0],
            recv_sem=sems.at[1],
            device_id={"clique": 0},
            device_id_type=MESH,
        ).wait_recv()

    for c in range(PIECES):
        outgoing[c] = arrived[info[SOURCE + c] % 4]
    send_received(me, outgoing, received, incoming, more_sems)

    @pl.when(me == 0)
    def _():
        pltpu.make_async_remote_copy(
            src_ref=margins.at[pl.ds(1, PIECES - 1)],
            dst_ref=margins.at[pl.ds(1, PIECES - 1)],
            send_sem=sems.at[0],
            recv_sem=sems.at[1],
            device_id={"clique": 1},
            device_id_type=MESH,
        ).wait_send()


def spread_kernel(info, margins, received, arrived, outgoing, incoming, sems, more_sems):
    me = lax.axis_index("clique")
    enter(me)
    send_pieces(me, margins, arrived, sems)
    arrived[me] = margins[me]
    all_but_one(me, margins, arrived, sems).wait_recv()
    for c in range(PIECES):
        outgoing[c] = arrived[info[SOURCE + c] // 4, info[SOURCE + c] % 4]
    send_received(me, outgoing, received, incoming, more_sems)
    all_but_one(me, margins, arrived, sems).wait_send()


MESSAGE = jax.ShapeDtypeStruct((PIECES, 8, 128), F32)
SLOTS = jax.ShapeDtypeStruct((PIECES, 4, 8, 128), F32)
TABLE = jax.ShapeDtypeStruct((1024, 1024), F32)
ANY_SPEC = pl.BlockSpec(memory_space=pl.ANY)
S_SPEC = pl.BlockSpec(memory_space=SMEM)
V_SPEC = pl.BlockSpec(memory_space=VMEM)
HELD_MESSAGE = VMEM((PIECES, 8, 128), F32)
HELD_SUMS = VMEM((PIECES + 1, 8, 128), F32)
HELD_SLOTS = VMEM((PIECES, 4, 8, 128), F32)
HELD_PIECE = VMEM((4, 8, 128), F32)
HELD_TABLE = VMEM((1024, 1024), F32)
WORK = [VMEM((1024, 128), F32), VMEM((1024, 128), F32), VMEM((8, 32, 128), F32)]
PAIR_SEMS = pltpu.SemaphoreType.DMA((2,))


def call(kernel, name, ins, outs, out_specs, scratch, collective=None, limit=20):
    more = {} if collective is None else dict(collective_id=collective, has_side_effects=True)
    return pl.pallas_call(
        kernel,
        name=name,
        in_specs=ins,
        out_shape=outs,
        out_specs=out_specs,
        scratch_shapes=scratch,
        compiler_params=pltpu.CompilerParams(vmem_limit_bytes=limit * 2**20, **more),
    )


def per_device(potentials, parent, child_drop, parent_drop):
    table = potentials.reshape(1024, 1024)
    trees = jnp.concatenate([child_drop, parent_drop, parent])
    message, info = call(
        first_kernel,
        "first",
        [ANY_SPEC] * 2,
        (MESSAGE, jax.ShapeDtypeStruct((INFO,), jnp.int32)),
        (V_SPEC, S_SPEC),
        [HELD_TABLE, SMEM((9, 32), jnp.int32)]
        + WORK
        + [pltpu.SemaphoreType.DMA((CHUNKS,)), pltpu.SemaphoreType.DMA],
        limit=53,
    )(trees, table)
    slots = call(
        sums_kernel,
        "sums",
        [S_SPEC, V_SPEC],
        SLOTS,
        V_SPEC,
        [HELD_MESSAGE, HELD_SUMS, HELD_SLOTS, HELD_SLOTS, PAIR_SEMS, PAIR_SEMS],
        collective=0,
    )(info, message)
    message = call(
        up_kernel, "up", [S_SPEC] + [V_SPEC] * 2, MESSAGE, V_SPEC, [HELD_TABLE] + WORK
    )(info, table, slots)
    slots = call(
        root_sums_kernel,
        "root_sums",
        [S_SPEC] + [V_SPEC] * 2,
        SLOTS,
        V_SPEC,
        [HELD_MESSAGE, HELD_SUMS, HELD_PIECE, HELD_SLOTS, PAIR_SEMS, PAIR_SEMS],
        collective=1,
    )(info, message, slots)
    axes = ("clique", "subtree")
    sent, table = call(
        chain_first_kernel, "chain_1", [S_SPEC] + [V_SPEC] * 2, (MESSAGE, TABLE), (V_SPEC, V_SPEC), WORK
    )(info, table, slots)
    first = lax.ppermute(sent, axes, ((3, 2), (0, 1)))
    sent = call(
        functools.partial(chain_kernel, 2),
        "chain_2",
        [S_SPEC] + [V_SPEC] * 2,
        MESSAGE,
        V_SPEC,
        [HELD_TABLE] + WORK,
    )(info, table, first)
    second = lax.ppermute(sent, axes, ((2, 1), (1, 2)))
    sent, table = call(
        functools.partial(chain_kernel, 3),
        "chain_3",
        [S_SPEC] + [V_SPEC] * 2,
        (MESSAGE, TABLE),
        (V_SPEC, V_SPEC),
        WORK,
    )(info, table, second)
    third = lax.ppermute(sent, axes, ((1, 0), (2, 3)))
    margins, table = call(
        root_margins_kernel,
        "root_margins",
        [S_SPEC] + [V_SPEC] * 3,
        (SLOTS, TABLE),
        (V_SPEC, V_SPEC),
        [HELD_MESSAGE] + WORK,
    )(info, table, first, third)
    received = call(
        root_spread_kernel,
        "root_spread",
        [S_SPEC, V_SPEC],
        MESSAGE,
        V_SPEC,
        [HELD_PIECE, HELD_MESSAGE, HELD_MESSAGE, PAIR_SEMS, PAIR_SEMS],
        collective=2,
    )(info, margins)
    margins = call(
        child_margins_kernel,
        "child_margins",
        [S_SPEC] + [V_SPEC] * 3,
        SLOTS,
        V_SPEC,
        [HELD_TABLE, HELD_MESSAGE] + WORK,
    )(info, table, received, message)
    received = call(
        spread_kernel,
        "spread",
        [S_SPEC, V_SPEC],
        MESSAGE,
        V_SPEC,
        [HELD_SLOTS, HELD_MESSAGE, HELD_MESSAGE, PAIR_SEMS, PAIR_SEMS],
        collective=3,
    )(info, margins)
    out = call(
        final_kernel,
        "final",
        [S_SPEC] + [V_SPEC] * 3,
        TABLE,
        ANY_SPEC,
        [HELD_TABLE, HELD_MESSAGE, pltpu.SemaphoreType.DMA((4,))],
    )(info, table, received, message)
    return out.reshape(1, 1, 1024, 1024)


def solution(mesh):
    specs = (P("subtree", "clique", None, None), P("subtree", None), P(), P())
    return jax.shard_map(
        per_device,
        mesh=mesh,
        in_specs=specs,
        out_specs=P("subtree", "clique", None, None),
        check_vma=False,
    )
```

time: 316 us -> 140 us (0.44)
  the two profiles are of different devices: /device:TPU:1 before, /device:TPU:6 now
where the time goes in v2:
time: 140 us
  Pallas kernels  124 us (89%)
  waiting for transfers between devices  9.56 us (7%)
  starting transfers between devices  5.8 us (4%)
    pallas_call x1, Pallas kernels, per_device(): call(sums_kernel, 'sums', [S_SPEC, V_SPEC], SLOTS, V_SPEC, [HELD_MESSAGE,...  21.3 us
    pallas_call x1, Pallas kernels, per_device(): call(spread_kernel, 'spread', [S_SPEC, V_SPEC], MESSAGE, V_SPEC, [HELD_SL...  18.4 us
    pallas_call x1, Pallas kernels, per_device(): call(root_sums_kernel, 'root_sums', [S_SPEC] + [V_SPEC] * 2, SLOTS, V_SPE...  15.3 us
    pallas_call x1, Pallas kernels, per_device(): call(root_spread_kernel, 'root_spread', [S_SPEC, V_SPEC], MESSAGE, V_SPEC...  14.2 us
    pallas_call x1, Pallas kernels, per_device(): call(child_margins_kernel, 'child_margins', [S_SPEC] + [V_SPEC] * 3, SLOT...  10.8 us
    pallas_call x1, Pallas kernels, per_device(): call(root_margins_kernel, 'root_margins', [S_SPEC] + [V_SPEC] * 3, (SLOTS...  10.7 us
    ppermute x1, waiting for transfers between devices, per_device(): third = lax.ppermute(sent, axes, ((1, 0), (2, 3)))  7.06 us
    pallas_call x1, Pallas kernels, per_device(): call(chain_first_kernel, 'chain_1', [S_SPEC] + [V_SPEC] * 2, (MESSAGE, TA...  5.97 us
  transfers between devices with their start and end apart: 3, of which 2 were waited for; matrix products, arithmetic and copies ran while one was open for 0% of the time, Pallas kernels for 0%

profile of v2, /device:TPU:6, one launch (start us, length us, event | category | flops | bytes accessed | tf_op | source)
XLA Modules:
  0.0 140.1 jit_solution(17210056786948628855)
XLA Ops:
  0.0 0.0 copy-start
  0.0 0.9 pad_add_fusion.trees_in
  0.9 4.8 %first.1 = (f32[32,8,128]{2,1,0:T(8,128)S(1)}, s32[256]{0:T(256)S(1)}) custom-call(s32[9,32]{1,0:T(8,128)S(1)} %pad_add_fusion.trees_in, f32[1024,1024]{1,0:T(8,128)} %bitcast.2), custom_call_target="tpu_custom_call" | custom-call | tf_op jit(solution)/shard_map/first/pallas_call | solution.py:559
  5.7 21.3 %sums.1.slots.old_slots = f32[32,4,8,128]{3,2,1,0:T(8,128)S(1)} custom-call(s32[256]{0:T(256)S(1)} %get-tuple-element.13.info, f32[32,8,128]{2,1,0:T(8,128)S(1)} %get-tuple-element.14.message), custom_call_target="tpu_custom_call" | custom-call | tf_op jit(solution)/shard_map/sums/pallas_call | solution.py:570
  27.0 0.0 copy-done
  27.0 6.0 %up.1.message = f32[32,8,128]{2,1,0:T(8,128)S(1)} custom-call(s32[256]{0:T(256)S(1)} %get-tuple-element.13.info, f32[1024,1024]{1,0:T(8,128)S(1)} %bitcast.3, f32[32,4,8,128]{3,2,1,0:T(8,128)S(1)} %sums.1.slots.old_slots), custom_call_target="tpu_custom_call" | custom-call | tf_op jit(solution)/shard_map/up/pallas_call | solution.py:579
  32.9 15.3 %root_sums.1.slots = f32[32,4,8,128]{3,2,1,0:T(8,128)S(1)} custom-call(s32[256]{0:T(256)S(1)} %get-tuple-element.13.info, f32[32,8,128]{2,1,0:T(8,128)S(1)} %up.1.message, f32[32,4,8,128]{3,2,1,0:T(8,128)S(1)} %sums.1.slots.old_slots), custom_call_target="tpu_custom_call" | custom-call | tf_op jit(solution)/shard_map/root_sums/pallas_call | solution.py:582
  48.3 6.0 %chain_1.1 = (f32[32,8,128]{2,1,0:T(8,128)S(1)}, f32[1024,1024]{1,0:T(8,128)S(1)}) custom-call(s32[256]{0:T(256)S(1)} %get-tuple-element.13.info, f32[1024,1024]{1,0:T(8,128)S(1)} %bitcast.4, f32[32,4,8,128]{3,2,1,0:T(8,128)S(1)} %root_sums.1.slots), custom_call_target="tpu_custom_call" | custom-call | tf_op jit(solution)/shard_map/chain_1/pallas_call | solution.py:592
  54.3 3.8 %collective-permute-start = (f32[32,8,128]{2,1,0:T(8,128)S(1)}, f32[32,8,128]{2,1,0:T(8,128)S(1)}, u32[]{:S(2)}, u32[]{:S(2)}) collective-permute-start(f32[32,8,128]{2,1,0:T(8,128)S(1)} %get-tuple-element.16), channel_id=1, source_target_pairs={{3,2},{0,1}} | collective-permute-start | bytes 393224 | tf_op jit(solution)/shard_map/ppermute | solution.py:595
  58.1 2.5 %collective-permute-done.arrived.first = f32[32,8,128]{2,1,0:T(8,128)S(1)} collective-permute-done((f32[32,8,128]{2,1,0:T(8,128)S(1)}, f32[32,8,128]{2,1,0:T(8,128)S(1)}, u32[]{:S(2)}, u32[]{:S(2)}) %collective-permute-start) | collective-permute-done | bytes 131104 | tf_op jit(solution)/shard_map/ppermute | solution.py:595
  60.6 5.6 %chain_2.1 = f32[32,8,128]{2,1,0:T(8,128)S(1)} custom-call(s32[256]{0:T(256)S(1)} %get-tuple-element.13.info, f32[1024,1024]{1,0:T(8,128)S(1)} %get-tuple-element.15.table, f32[32,8,128]{2,1,0:T(8,128)S(1)} %collective-permute-done.arrived.first), custom_call_target="tpu_custom_call" | custom-call | tf_op jit(solution)/shard_map/chain_2/pallas_call | solution.py:596
  66.2 0.7 collective-permute-start.1
  66.9 0.0 collective-permute-done.1.arrived
  66.9 5.6 %chain_3.1 = (f32[32,8,128]{2,1,0:T(8,128)S(1)}, f32[1024,1024]{1,0:T(8,128)S(1)}) custom-call(s32[256]{0:T(256)S(1)} %get-tuple-element.13.info, f32[1024,1024]{1,0:T(8,128)S(1)} %get-tuple-element.15.table, f32[32,8,128]{2,1,0:T(8,128)S(1)} %collective-permute-done.1.arrived), custom_call_target="tpu_custom_call" | custom-call | tf_op jit(solution)/shard_map/chain_3/pallas_call | solution.py:605
  72.4 1.3 collective-permute-start.2
  73.7 7.1 %collective-permute-done.2.third = f32[32,8,128]{2,1,0:T(8,128)S(1)} collective-permute-done((f32[32,8,128]{2,1,0:T(8,128)S(1)}, f32[32,8,128]{2,1,0:T(8,128)S(1)}, u32[]{:S(2)}, u32[]{:S(2)}) %collective-permute-start.2) | collective-permute-done | bytes 131104 | tf_op jit(solution)/shard_map/ppermute | solution.py:613
  80.8 10.7 %root_margins.1 = (f32[32,4,8,128]{3,2,1,0:T(8,128)S(1)}, f32[1024,1024]{1,0:T(8,128)S(1)}) custom-call(s32[256]{0:T(256)S(1)} %get-tuple-element.13.info, f32[1024,1024]{1,0:T(8,128)S(1)} %get-tuple-element.17.table, f32[32,8,128]{2,1,0:T(8,128)S(1)} %collective-permute-done.arrived.first, f32[32,8,128]{2,1,0:T(8,128)S(1)} %collective-permute-done.2.third), custom_call_target="tpu_custom_call" | custom-call | tf_op jit(solution)/shard_map/root_margins/pallas_call | solution.py:614
  91.5 14.2 %root_spread.1.received = f32[32,8,128]{2,1,0:T(8,128)S(1)} custom-call(s32[256]{0:T(256)S(1)} %get-tuple-element.13.info, f32[32,4,8,128]{3,2,1,0:T(8,128)S(1)} %get-tuple-element.20.margins), custom_call_target="tpu_custom_call" | custom-call | tf_op jit(solution)/shard_map/root_spread/pallas_call | solution.py:622
  105.7 10.8 %child_margins.1.margins = f32[32,4,8,128]{3,2,1,0:T(8,128)S(1)} custom-call(s32[256]{0:T(256)S(1)} %get-tuple-element.13.info, f32[1024,1024]{1,0:T(8,128)S(1)} %get-tuple-element.19.table, f32[32,8,128]{2,1,0:T(8,128)S(1)} %root_spread.1.received, f32[32,8,128]{2,1,0:T(8,128)S(1)} %up.1.message), custom_call_target="tpu_custom_call" | custom-call | tf_op jit(solution)/shard_map/child_margins/pallas_call | solution.py:631
  116.5 18.4 %spread.1.received = f32[32,8,128]{2,1,0:T(8,128)S(1)} custom-call(s32[256]{0:T(256)S(1)} %get-tuple-element.13.info, f32[32,4,8,128]{3,2,1,0:T(8,128)S(1)} %child_margins.1.margins), custom_call_target="tpu_custom_call" | custom-call | tf_op jit(solution)/shard_map/spread/pallas_call | solution.py:639
  134.9 5.1 %final.1 = f32[1024,1024]{1,0:T(8,128)} custom-call(s32[256]{0:T(256)S(1)} %get-tuple-element.13.info, f32[1024,1024]{1,0:T(8,128)S(1)} %get-tuple-element.19.table, f32[32,8,128]{2,1,0:T(8,128)S(1)} %spread.1.received, f32[32,8,128]{2,1,0:T(8,128)S(1)} %up.1.message), custom_call_target="tpu_custom_call" | custom-call | tf_op jit(solution)/shard_map/final/pallas_call | solution.py:648
Async XLA Ops:
  0.0 27.0 %copy-start = (f32[1,1,1024,1024]{3,2,1,0:T(8,128)S(1)}, f32[1,1,1024,1024]{3,2,1,0:T(8,128)}, u32[]{:S(2)}) copy-start(f32[1,1,1024,1024]{3,2,1,0:T(8,128)} %param.4) | copy-start | bytes 12582916
  54.3 6.3 %collective-permute-start = (f32[32,8,128]{2,1,0:T(8,128)S(1)}, f32[32,8,128]{2,1,0:T(8,128)S(1)}, u32[]{:S(2)}, u32[]{:S(2)}) collective-permute-start(f32[32,8,128]{2,1,0:T(8,128)S(1)} %get-tuple-element.16), channel_id=1, source_target_pairs={{3,2},{0,1}} | collective-permute-start | bytes 393224 | tf_op jit(solution)/shard_map/ppermute | solution.py:595
  66.2 0.7 collective-permute-start.1
  72.4 8.4 %collective-permute-start.2 = (f32[32,8,128]{2,1,0:T(8,128)S(1)}, f32[32,8,128]{2,1,0:T(8,128)S(1)}, u32[]{:S(2)}, u32[]{:S(2)}) collective-permute-start(f32[32,8,128]{2,1,0:T(8,128)S(1)} %get-tuple-element.18), channel_id=1, source_target_pairs={{1,0},{2,3}} | collective-permute-start | bytes 393224 | tf_op jit(solution)/shard_map/ppermute | solution.py:613

commit v3 on v2

--- a/solution.py
+++ b/solution.py
@@ -38,38 +38,66 @@
     return table[pl.ds(pl.multiple_of(a0 * 32 + 8 * i, 8), 8), 128 * t : 128 * (t + 1)]
 
 
-def place(source, target, terms, after=None):
+def prepare_place(hot):
+    row = lax.broadcasted_iota(jnp.int32, (256, 1024), 0)
+    column = lax.broadcasted_iota(jnp.int32, (256, 1024), 1)
+    level = jnp.where(row < 128, column // 32, column % 32)
+    hot[...] = jnp.where((level == row % 32) & (row % 128 < 96), 1.0, 0.0).astype(jnp.bfloat16)
+
+
+def three_parts(vec):
+    high = vec.astype(jnp.bfloat16).astype(F32)
+    rest = vec - high
+    middle = rest.astype(jnp.bfloat16).astype(F32)
+    group = lanes() // 32
+    return jnp.where(group == 0, high, jnp.where(group == 1, middle, jnp.where(group == 2, rest - middle, 0.0)))
+
+
+def place(source, target, terms, tools, after=None):
+    left, hot = tools
     lane, row = lanes(), rows()
-    spread_third = (row % 4) * 32 + lane % 32
-    spread_fourth = [(row % 4) * 32 + lane // 32 + 4 * t for t in range(8)]
+    spread = (row % 4) * 32 + lane % 32
+    by_matrix = [k for k in (3, 2) if k in terms] if 3 in terms else []
+    depth = 128 * len(by_matrix)
 
     def body(part, carry):
-        for s in range(8):
-            a0 = part * 8 + s
-
-            def slot_row(k, j):
-                return terms[k][1](part * 8 + j, s)
-
-            second = [slot_row(1, t) for t in range(8)] if 1 in terms else None
-            for i in range(4):
-                both = {
-                    k: jnp.where(row < 4, slot_row(k, 2 * i), slot_row(k, 2 * i + 1))
-                    for k in (2, 3)
-                    if k in terms
-                }
-                third = take(both[2], spread_third) if 2 in terms else None
-                for t in range(8):
-                    adds = [tile(source, a0, i, t)]
-                    if 0 in terms:
-                        adds.append(terms[0][0](i * 8 + t))
-                    if 1 in terms:
-                        adds.append(jnp.broadcast_to(second[t], (8, 128)))
-                    if 2 in terms:
-                        adds.append(third)
-                    if 3 in terms:
-                        adds.append(take(both[3], spread_fourth[t]))
-                    where = pl.ds(pl.multiple_of(a0 * 32 + 8 * i, 8), 8)
-                    target[where, 128 * t : 128 * (t + 1)] = tree(adds, jnp.add)
+        def levels(k, s, i):
+            read = terms[k][1]
+            return take(jnp.where(row < 4, read(part * 8 + 2 * i, s), read(part * 8 + 2 * i + 1, s)), spread)
+
+        if by_matrix:
+            for s in range(8):
+                for half in range(2):
+                    both = [
+                        jnp.concatenate([three_parts(levels(k, s, i)) for k in by_matrix], axis=1)
+                        for i in (2 * half, 2 * half + 1)
+                    ]
+                    at = 32 * s + 16 * half
+                    left[at : at + 16, :depth] = jnp.concatenate(both, axis=0).astype(jnp.bfloat16)
+        for n in range(4):
+            if by_matrix:
+                back = jnp.dot(
+                    left[:, :depth], hot[:depth, 256 * n : 256 * (n + 1)], preferred_element_type=F32
+                )
+            for s in range(8):
+                a0 = part * 8 + s
+                third = [levels(2, s, i) for i in range(4)] if 2 in terms and not by_matrix else None
+                for t in (2 * n, 2 * n + 1):
+                    second = terms[1][1](part * 8 + t, s) if 1 in terms else None
+                    for i in range(4):
+                        adds = []
+                        if 0 in terms:
+                            adds.append(terms[0][0](i * 8 + t))
+                        if 1 in terms:
+                            adds.append(jnp.broadcast_to(second, (8, 128)))
+                        if third is not None:
+                            adds.append(third[i])
+                        if by_matrix:
+                            at, column = 32 * s + 8 * i, 128 * (t - 2 * n)
+                            adds.append(back[at : at + 8, column : column + 128])
+                        where = pl.ds(pl.multiple_of(a0 * 32 + 8 * i, 8), 8)
+                        value = tile(source, a0, i, t) + functools.reduce(jnp.add, adds)
+                        target[where, 128 * t : 128 * (t + 1)] = value
         if after is not None:
             after(part)
         return carry
@@ -77,20 +105,23 @@
     lax.fori_loop(0, 4, body, 0)
 
 
-def place_slots(source, target, slots, after=None):
+def place_slots(source, target, slots, tools, after=None):
     def readers(k):
         return lambda piece: slots[piece, k], lambda piece, s: slots[piece, k, pl.ds(s, 1), :]
 
-    place(source, target, {k: readers(k) for k in range(4)}, after)
-
-
-def place_message(source, target, message, axis, after=None):
+    prepare_place(tools[1])
+    place(source, target, {k: readers(k) for k in range(4)}, tools, after)
+
+
+def place_message(source, target, message, axis, tools, after=None):
     for k in range(4):
 
         @pl.when(axis == k)
         def _(k=k):
             readers = (lambda piece: message[piece], lambda piece, s: message[piece, pl.ds(s, 1), :])
-            place(source, target, {k: readers}, after)
+            if k == 3:
+                prepare_place(tools[1])
+            place(source, target, {k: readers}, tools, after)
 
 
 def pick(parts):
@@ -246,7 +277,7 @@
 
 
 def first_kernel(trees_in, potentials, message, info, table, trees, *rest):
-    work, load_sems, sems = rest[:3], rest[3], rest[4]
+    work, load_sems, sems = rest[:5], rest[5], rest[6]
     me, s = lax.axis_index("clique"), lax.axis_index("subtree")
     size = 1024 // CHUNKS
     loads = [
@@ -286,68 +317,47 @@
 
 
 def up_kernel(info, table, slots, message, placed, *work):
-    place_slots(table, placed, slots)
+    place_slots(table, placed, slots, work[3:])
     chosen_margin(placed, info[OWN_DROP], message, work)
 
 
 def chain_first_kernel(info, table, slots, message, placed, *work):
-    place_slots(table, placed, slots)
+    place_slots(table, placed, slots, work[3:])
     chosen_margin(placed, info[CHAIN_AXIS + 1], message, work)
 
 
 def chain_kernel(step, info, table, arrived, message, placed, *work):
-    place_message(table, placed, arrived, info[CHAIN_SLOT + step - 1])
+    place_message(table, placed, arrived, info[CHAIN_SLOT + step - 1], work[3:])
     chosen_margin(placed, info[CHAIN_AXIS + step], message, work)
 
 
-def all_margins(table, margins, work):
-    for k in range(4):
-        MARGINS[k](table, slot_put(margins, k), work)
-
-
-def root_margins_kernel(info, table, first, third, margins, belief, held, *work):
+def last_root_slot(info):
     s = lax.axis_index("subtree")
     inner = (s == 1) | (s == 2)
-
-    def body(piece, carry):
-        held[piece] = jnp.where(inner, first[piece], third[piece])
-        return carry
-
-    lax.fori_loop(0, PIECES, body, 0)
-    place_message(table, belief, held, jnp.where(inner, info[CHAIN_SLOT + 1], info[CHAIN_SLOT + 3]))
-    all_margins(belief, margins, work)
-
-
-def child_margins_kernel(info, table, received, message, margins, belief, held, *work):
+    return inner, jnp.where(inner, info[CHAIN_SLOT + 1], info[CHAIN_SLOT + 3])
+
+
+def final_kernel(info, table, first, third, received, message, out, belief, held, left, hot, sems):
     below = lax.axis_index("clique") != 0
-
-    def body(piece, carry):
-        held[piece] = jnp.where(below, received[piece] - message[piece], 0.0)
-        return carry
-
-    lax.fori_loop(0, PIECES, body, 0)
-    place_message(table, belief, held, info[OWN_DROP])
-    all_margins(belief, margins, work)
-
-
-def final_kernel(info, table, received, message, out, belief, held, sems):
-    below = lax.axis_index("clique") != 0
+    inner, slot = last_root_slot(info)
     top = jnp.max(tree([received[piece] for piece in range(PIECES)], jnp.maximum))
     total = tree([jnp.exp(received[piece] - top) for piece in range(PIECES)], jnp.add)
     log_total = top + jnp.log(jnp.broadcast_to(jnp.sum(total), (8, 128)))
     for piece in range(PIECES):
-        held[piece] = jnp.where(below, received[piece] - message[piece], 0.0) - log_total
+        at_root = jnp.where(inner, first[piece], third[piece])
+        held[piece] = jnp.where(below, received[piece] - message[piece], at_root) - log_total
 
     def out_copy(part):
         at = pl.ds(pl.multiple_of(part * 256, 256), 256)
         return pltpu.make_async_copy(belief.at[at], out.at[at], sems.at[part])
 
-    place_message(table, belief, held, info[OWN_DROP], after=lambda part: out_copy(part).start())
+    axis = jnp.where(below, info[OWN_DROP], slot)
+    place_message(table, belief, held, axis, (left, hot), after=lambda part: out_copy(part).start())
     for part in range(4):
         out_copy(part).wait()
 
 
-def enter(me):
+def announce(me):
     barrier = pltpu.get_barrier_semaphore()
 
     def body(d, carry):
@@ -355,7 +365,15 @@
         return carry
 
     lax.fori_loop(1, PIECES, body, 0)
-    pl.semaphore_wait(barrier, PIECES - 1)
+
+
+def await_others():
+    pl.semaphore_wait(pltpu.get_barrier_semaphore(), PIECES - 1)
+
+
+def enter(me):
+    announce(me)
+    await_others()
 
 
 def send_pieces(me, source, target, sems):
@@ -453,76 +471,113 @@
         lax.fori_loop(1, PIECES, body, 0)
 
 
-def send_received(me, outgoing, received, incoming, sems):
-    send_pieces(me, outgoing, incoming, sems)
-    incoming[me] = outgoing[me]
-    all_but_one(me, outgoing, incoming, sems).wait()
-
-    def body(piece, carry):
-        received[piece] = incoming[piece]
-        return carry
-
-    lax.fori_loop(0, PIECES, body, 0)
-
-
-def root_spread_kernel(info, margins, received, arrived, outgoing, incoming, sems, more_sems):
-    me = lax.axis_index("clique")
-    enter(me)
-
-    @pl.when(me == 0)
-    def _():
-        def body(other, carry):
-            pltpu.make_async_remote_copy(
-                src_ref=margins.at[other],
-                dst_ref=arrived,
-                send_sem=sems.at[0],
-                recv_sem=sems.at[1],
-                device_id={"clique": other},
-                device_id_type=MESH,
-            ).start()
-            return carry
-
-        lax.fori_loop(1, PIECES, body, 0)
-        for k in range(4):
-            arrived[k] = margins[0, k]
-
-    @pl.when(me != 0)
-    def _():
+def send_slot(me, k, source, target, sems):
+    def body(d, carry):
+        other = (me + d) % PIECES
         pltpu.make_async_remote_copy(
-            src_ref=arrived,
-            dst_ref=arrived,
+            src_ref=source.at[other, k],
+            dst_ref=target.at[me, k],
             send_sem=sems.at[0],
             recv_sem=sems.at[1],
-            device_id={"clique": 0},
+            device_id={"clique": other},
             device_id_type=MESH,
-        ).wait_recv()
+        ).start()
+        return carry
+
+    lax.fori_loop(1, PIECES, body, 0)
+
+
+def part_of(me, count, source, target, sems):
+    return pltpu.make_async_remote_copy(
+        src_ref=source.at[pl.ds(0, count)],
+        dst_ref=target.at[pl.ds(0, count)],
+        send_sem=sems.at[0],
+        recv_sem=sems.at[1],
+        device_id={"clique": (me + 1) % PIECES},
+        device_id_type=MESH,
+    )
+
+
+def down_kernel(info, table, first, third, message, received, *scratch):
+    belief, margins, held, arrived, out_1, in_1, out_2, in_2 = scratch[:8]
+    work, sems = scratch[8:13], scratch[13:]
+    me = lax.axis_index("clique")
+    announce(me)
+
+    def send_margins(pair):
+        for k in (2, 1, 3, 0):
+            MARGINS[k](belief, slot_put(margins, k), work)
+            send_slot(me, k, margins, arrived, pair)
+        for k in range(4):
+            arrived[me, k] = margins[me, k]
+
+    @pl.when(me == 0)
+    def _():
+        inner, slot = last_root_slot(info)
+
+        def body(piece, carry):
+            value = jnp.where(inner, first[piece], third[piece])
+            for k in range(4):
+                held[piece, k] = jnp.where(slot == k, value, 0.0)
+            return carry
+
+        lax.fori_loop(0, PIECES, body, 0)
+        place_slots(table, belief, held, work[3:])
+
+    await_others()
+
+    @pl.when(me == 0)
+    def _():
+        send_margins(sems[0])
+
+    @pl.when(me != 0)
+    def _():
+        part_of(me, 1, margins, arrived, sems[0]).wait_recv()
 
     for c in range(PIECES):
-        outgoing[c] = arrived[info[SOURCE + c] % 4]
-    send_received(me, outgoing, received, incoming, more_sems)
+        out_1[c] = arrived[0, info[SOURCE + c] % 4]
+    send_pieces(me, out_1, in_1, sems[1])
+    in_1[me] = out_1[me]
+    all_but_one(me, out_1, in_1, sems[1]).wait()
+
+    @pl.when(me != 0)
+    def _():
+        drop = info[OWN_DROP]
+
+        def body(piece, carry):
+            value = in_1[piece] - message[piece]
+            for k in range(4):
+                held[piece, k] = jnp.where(drop == k, value, 0.0)
+            return carry
+
+        lax.fori_loop(0, PIECES, body, 0)
+        place_slots(table, belief, held, work[3:])
+        send_margins(sems[2])
+        part_of(me, PIECES - 2, margins, arrived, sems[2]).wait_recv()
 
     @pl.when(me == 0)
     def _():
-        pltpu.make_async_remote_copy(
-            src_ref=margins.at[pl.ds(1, PIECES - 1)],
-            dst_ref=margins.at[pl.ds(1, PIECES - 1)],
-            send_sem=sems.at[0],
-            recv_sem=sems.at[1],
-            device_id={"clique": 1},
-            device_id_type=MESH,
-        ).wait_send()
-
-
-def spread_kernel(info, margins, received, arrived, outgoing, incoming, sems, more_sems):
-    me = lax.axis_index("clique")
-    enter(me)
-    send_pieces(me, margins, arrived, sems)
-    arrived[me] = margins[me]
-    all_but_one(me, margins, arrived, sems).wait_recv()
+        part_of(me, PIECES - 1, margins, arrived, sems[2]).wait_recv()
+
     for c in range(PIECES):
-        outgoing[c] = arrived[info[SOURCE + c] // 4, info[SOURCE + c] % 4]
-    send_received(me, outgoing, received, incoming, more_sems)
-    all_but_one(me, margins, arrived, sems).wait_send()
+        out_2[c] = arrived[info[SOURCE + c] // 4, info[SOURCE + c] % 4]
+    send_pieces(me, out_2, in_2, sems[3])
+    in_2[me] = out_2[me]
+    all_but_one(me, out_2, in_2, sems[3]).wait()
+
+    def body(piece, carry):
+        received[piece] = in_2[piece]
+        return carry
+
+    lax.fori_loop(0, PIECES, body, 0)
+
+    @pl.when(me == 0)
+    def _():
+        part_of(me, PIECES - 1, margins, arrived, sems[0]).wait_send()
+
+    @pl.when(me != 0)
+    def _():
+        part_of(me, PIECES - 1, margins, arrived, sems[2]).wait_send()
 
 
 MESSAGE = jax.ShapeDtypeStruct((PIECES, 8, 128), F32)
@@ -536,7 +591,8 @@
 HELD_SLOTS = VMEM((PIECES, 4, 8, 128), F32)
 HELD_PIECE = VMEM((4, 8, 128), F32)
 HELD_TABLE = VMEM((1024, 1024), F32)
-WORK = [VMEM((1024, 128), F32), VMEM((1024, 128), F32), VMEM((8, 32, 128), F32)]
+PLACE_TOOLS = [VMEM((256, 256), jnp.bfloat16), VMEM((256, 1024), jnp.bfloat16)]
+WORK = [VMEM((1024, 128), F32), VMEM((1024, 128), F32), VMEM((8, 32, 128), F32)] + PLACE_TOOLS
 PAIR_SEMS = pltpu.SemaphoreType.DMA((2,))
 
 
@@ -611,48 +667,23 @@
         WORK,
     )(info, table, second)
     third = lax.ppermute(sent, axes, ((1, 0), (2, 3)))
-    margins, table = call(
-        root_margins_kernel,
-        "root_margins",
-        [S_SPEC] + [V_SPEC] * 3,
-        (SLOTS, TABLE),
-        (V_SPEC, V_SPEC),
-        [HELD_MESSAGE] + WORK,
-    )(info, table, first, third)
     received = call(
-        root_spread_kernel,
-        "root_spread",
-        [S_SPEC, V_SPEC],
+        down_kernel,
+        "down",
+        [S_SPEC] + [V_SPEC] * 4,
         MESSAGE,
         V_SPEC,
-        [HELD_PIECE, HELD_MESSAGE, HELD_MESSAGE, PAIR_SEMS, PAIR_SEMS],
+        [HELD_TABLE] + [HELD_SLOTS] * 3 + [HELD_MESSAGE] * 4 + WORK + [PAIR_SEMS] * 4,
         collective=2,
-    )(info, margins)
-    margins = call(
-        child_margins_kernel,
-        "child_margins",
-        [S_SPEC] + [V_SPEC] * 3,
-        SLOTS,
-        V_SPEC,
-        [HELD_TABLE, HELD_MESSAGE] + WORK,
-    )(info, table, received, message)
-    received = call(
-        spread_kernel,
-        "spread",
-        [S_SPEC, V_SPEC],
-        MESSAGE,
-        V_SPEC,
-        [HELD_SLOTS, HELD_MESSAGE, HELD_MESSAGE, PAIR_SEMS, PAIR_SEMS],
-        collective=3,
-    )(info, margins)
+    )(info, table, first, third, message)
     out = call(
         final_kernel,
         "final",
-        [S_SPEC] + [V_SPEC] * 3,
+        [S_SPEC] + [V_SPEC] * 5,
         TABLE,
         ANY_SPEC,
-        [HELD_TABLE, HELD_MESSAGE, pltpu.SemaphoreType.DMA((4,))],
-    )(info, table, received, message)
+        [HELD_TABLE, HELD_MESSAGE] + PLACE_TOOLS + [pltpu.SemaphoreType.DMA((4,))],
+    )(info, table, first, third, received, message)
     return out.reshape(1, 1, 1024, 1024)
 
 

time: 140 us -> 124 us (0.89)
  the two profiles are of different devices: /device:TPU:6 before, /device:TPU:1 now
where the time goes in v3:
time: 124 us
  Pallas kernels  120 us (97%)
  starting transfers between devices  2.01 us (2%)
    pallas_call x1, Pallas kernels, per_device(): call(down_kernel, 'down', [S_SPEC] + [V_SPEC] * 4, MESSAGE, V_SPEC, [HELD...  63.4 us
    pallas_call x1, Pallas kernels, per_device(): call(sums_kernel, 'sums', [S_SPEC, V_SPEC], SLOTS, V_SPEC, [HELD_MESSAGE,...  22.1 us
    pallas_call x1, Pallas kernels, per_device(): call(root_sums_kernel, 'root_sums', [S_SPEC] + [V_SPEC] * 2, SLOTS, V_SPE...  10.3 us
    pallas_call x1, Pallas kernels, per_device(): call(first_kernel, 'first', [ANY_SPEC] * 2, (MESSAGE, jax.ShapeDtypeStruc...  5.16 us
    pallas_call x1, Pallas kernels, per_device(): call(chain_first_kernel, 'chain_1', [S_SPEC] + [V_SPEC] * 2, (MESSAGE, TA...  4.52 us
    pallas_call x1, Pallas kernels, per_device(): call(up_kernel, 'up', [S_SPEC] + [V_SPEC] * 2, MESSAGE, V_SPEC, [HELD_TAB...  4.5 us
    pallas_call x1, Pallas kernels, per_device(): call(functools.partial(chain_kernel, 3), 'chain_3', [S_SPEC] + [V_SPEC] *...  3.66 us
    pallas_call x1, Pallas kernels, per_device(): call(functools.partial(chain_kernel, 2), 'chain_2', [S_SPEC] + [V_SPEC] *...  3.65 us
  transfers between devices with their start and end apart: 3, of which 0 were waited for; matrix products, arithmetic and copies ran while one was open for 0% of the time, Pallas kernels for 0%

profile of v3, /device:TPU:1, one launch (start us, length us, event | category | flops | bytes accessed | tf_op | source)
XLA Modules:
  0.0 123.6 jit_solution(12247519459824624574)
XLA Ops:
  0.0 0.0 copy-start
  0.0 0.9 pad_add_fusion.trees_in
  0.9 5.2 %first.1 = (f32[32,8,128]{2,1,0:T(8,128)S(1)}, s32[256]{0:T(256)S(1)}) custom-call(s32[9,32]{1,0:T(8,128)S(1)} %pad_add_fusion.trees_in, f32[1024,1024]{1,0:T(8,128)} %bitcast.2), custom_call_target="tpu_custom_call" | custom-call | tf_op jit(solution)/shard_map/first/pallas_call | solution.py:615
  6.0 22.1 %sums.1.slots.old_slots = f32[32,4,8,128]{3,2,1,0:T(8,128)S(1)} custom-call(s32[256]{0:T(256)S(1)} %get-tuple-element.11.info, f32[32,8,128]{2,1,0:T(8,128)S(1)} %get-tuple-element.12.message), custom_call_target="tpu_custom_call" | custom-call | tf_op jit(solution)/shard_map/sums/pallas_call | solution.py:626
  28.1 0.0 copy-done
  28.1 4.5 %up.1.message = f32[32,8,128]{2,1,0:T(8,128)S(1)} custom-call(s32[256]{0:T(256)S(1)} %get-tuple-element.11.info, f32[1024,1024]{1,0:T(8,128)S(1)} %bitcast.3, f32[32,4,8,128]{3,2,1,0:T(8,128)S(1)} %sums.1.slots.old_slots), custom_call_target="tpu_custom_call" | custom-call | tf_op jit(solution)/shard_map/up/pallas_call | solution.py:635
  32.7 10.3 %root_sums.1.slots = f32[32,4,8,128]{3,2,1,0:T(8,128)S(1)} custom-call(s32[256]{0:T(256)S(1)} %get-tuple-element.11.info, f32[32,8,128]{2,1,0:T(8,128)S(1)} %up.1.message, f32[32,4,8,128]{3,2,1,0:T(8,128)S(1)} %sums.1.slots.old_slots), custom_call_target="tpu_custom_call" | custom-call | tf_op jit(solution)/shard_map/root_sums/pallas_call | solution.py:638
  43.0 4.5 %chain_1.1 = (f32[32,8,128]{2,1,0:T(8,128)S(1)}, f32[1024,1024]{1,0:T(8,128)S(1)}) custom-call(s32[256]{0:T(256)S(1)} %get-tuple-element.11.info, f32[1024,1024]{1,0:T(8,128)S(1)} %bitcast.4, f32[32,4,8,128]{3,2,1,0:T(8,128)S(1)} %root_sums.1.slots), custom_call_target="tpu_custom_call" | custom-call | tf_op jit(solution)/shard_map/chain_1/pallas_call | solution.py:648
  47.5 0.7 collective-permute-start
  48.2 0.0 collective-permute-done.arrived.first
  48.2 3.7 %chain_2.1 = f32[32,8,128]{2,1,0:T(8,128)S(1)} custom-call(s32[256]{0:T(256)S(1)} %get-tuple-element.11.info, f32[1024,1024]{1,0:T(8,128)S(1)} %get-tuple-element.13.table, f32[32,8,128]{2,1,0:T(8,128)S(1)} %collective-permute-done.arrived.first), custom_call_target="tpu_custom_call" | custom-call | tf_op jit(solution)/shard_map/chain_2/pallas_call | solution.py:652
  51.9 0.7 collective-permute-start.1
  52.5 0.0 collective-permute-done.1.arrived
  52.6 3.7 %chain_3.1 = (f32[32,8,128]{2,1,0:T(8,128)S(1)}, f32[1024,1024]{1,0:T(8,128)S(1)}) custom-call(s32[256]{0:T(256)S(1)} %get-tuple-element.11.info, f32[1024,1024]{1,0:T(8,128)S(1)} %get-tuple-element.13.table, f32[32,8,128]{2,1,0:T(8,128)S(1)} %collective-permute-done.1.arrived), custom_call_target="tpu_custom_call" | custom-call | tf_op jit(solution)/shard_map/chain_3/pallas_call | solution.py:661
  56.2 0.7 collective-permute-start.2
  56.9 0.0 collective-permute-done.2.third
  56.9 63.4 %down.1.received = f32[32,8,128]{2,1,0:T(8,128)S(1)} custom-call(s32[256]{0:T(256)S(1)} %get-tuple-element.11.info, f32[1024,1024]{1,0:T(8,128)S(1)} %get-tuple-element.15.table, f32[32,8,128]{2,1,0:T(8,128)S(1)} %collective-permute-done.arrived.first, f32[32,8,128]{2,1,0:T(8,128)S(1)} %collective-permute-done.2.third, f32[32,8,128]{2,1,0:T(8,128)S(1)} %up.1.message), custom_call_target="tpu_custom_call" | custom-call | tf_op jit(solution)/shard_map/down/pallas_call | solution.py:670
  120.3 3.1 %final.1 = f32[1024,1024]{1,0:T(8,128)} custom-call(s32[256]{0:T(256)S(1)} %get-tuple-element.11.info, f32[1024,1024]{1,0:T(8,128)S(1)} %get-tuple-element.15.table, f32[32,8,128]{2,1,0:T(8,128)S(1)} %collective-permute-done.arrived.first, f32[32,8,128]{2,1,0:T(8,128)S(1)} %collective-permute-done.2.third, f32[32,8,128]{2,1,0:T(8,128)S(1)} %down.1.received, ...), custom_call_target="tpu_custom_call" | custom-call | tf_op jit(solution)/shard_map/final/pallas_call | solution.py:679
Async XLA Ops:
  0.0 28.1 %copy-start = (f32[1,1,1024,1024]{3,2,1,0:T(8,128)S(1)}, f32[1,1,1024,1024]{3,2,1,0:T(8,128)}, u32[]{:S(2)}) copy-start(f32[1,1,1024,1024]{3,2,1,0:T(8,128)} %param.4) | copy-start | bytes 12582916
  47.5 0.7 collective-permute-start
  51.9 0.7 collective-permute-start.1
  56.2 0.7 collective-permute-start.2

commit v4 on v3

--- a/solution.py
+++ b/solution.py
@@ -105,11 +105,12 @@
     lax.fori_loop(0, 4, body, 0)
 
 
-def place_slots(source, target, slots, tools, after=None):
+def place_slots(source, target, slots, tools, after=None, prepared=False):
     def readers(k):
         return lambda piece: slots[piece, k], lambda piece, s: slots[piece, k, pl.ds(s, 1), :]
 
-    prepare_place(tools[1])
+    if not prepared:
+        prepare_place(tools[1])
     place(source, target, {k: readers(k) for k in range(4)}, tools, after)
 
 
@@ -309,7 +310,8 @@
     to_next = trees[4 + jnp.minimum(s + 1, 3), 0]
     to_previous = trees[s, 0]
     for step, sender, receiver in ((1, 0, 2), (2, 1, 1), (3, 2, 0)):
-        info[CHAIN_AXIS + step] = jnp.where(s == sender, to_next, to_previous)
+        active = (me == 0) & (((s == 1) | (s == 2)) == (step > 1))
+        info[CHAIN_AXIS + step] = jnp.where(active, jnp.where(s == sender, to_next, to_previous), 4)
         info[CHAIN_SLOT + step] = jnp.where(s == receiver, to_next, to_previous)
     for copy in loads:
         copy.wait()
@@ -331,40 +333,48 @@
     chosen_margin(placed, info[CHAIN_AXIS + step], message, work)
 
 
+def inner_root(s):
+    return (s == 1) | (s == 2)
+
+
 def last_root_slot(info):
-    s = lax.axis_index("subtree")
-    inner = (s == 1) | (s == 2)
-    return inner, jnp.where(inner, info[CHAIN_SLOT + 1], info[CHAIN_SLOT + 3])
-
-
-def final_kernel(info, table, first, third, received, message, out, belief, held, left, hot, sems):
+    inner = inner_root(lax.axis_index("subtree"))
+    return jnp.where(inner, info[CHAIN_SLOT + 1], info[CHAIN_SLOT + 3])
+
+
+def final_kernel(info, table, last_root, received, message, out, belief, held, left, hot, sems):
     below = lax.axis_index("clique") != 0
-    inner, slot = last_root_slot(info)
     top = jnp.max(tree([received[piece] for piece in range(PIECES)], jnp.maximum))
     total = tree([jnp.exp(received[piece] - top) for piece in range(PIECES)], jnp.add)
     log_total = top + jnp.log(jnp.broadcast_to(jnp.sum(total), (8, 128)))
     for piece in range(PIECES):
-        at_root = jnp.where(inner, first[piece], third[piece])
-        held[piece] = jnp.where(below, received[piece] - message[piece], at_root) - log_total
+        held[piece] = jnp.where(below, received[piece] - message[piece], last_root[piece]) - log_total
 
     def out_copy(part):
         at = pl.ds(pl.multiple_of(part * 256, 256), 256)
         return pltpu.make_async_copy(belief.at[at], out.at[at], sems.at[part])
 
-    axis = jnp.where(below, info[OWN_DROP], slot)
+    axis = jnp.where(below, info[OWN_DROP], last_root_slot(info))
     place_message(table, belief, held, axis, (left, hot), after=lambda part: out_copy(part).start())
     for part in range(4):
         out_copy(part).wait()
 
 
+TURNS = sorted(
+    (turn for turn in range(1, PIECES)),
+    key=lambda turn: -(min(turn // 8, 4 - turn // 8) + min(turn // 2 % 4, 4 - turn // 2 % 4)),
+)
+
+
+def turned(me, turn):
+    y, z, core = (me // 8 + turn // 8) % 4, (me // 2 % 4 + turn // 2 % 4) % 4, (me % 2 + turn % 2) % 2
+    return y * 8 + z * 2 + core
+
+
 def announce(me):
     barrier = pltpu.get_barrier_semaphore()
-
-    def body(d, carry):
-        pl.semaphore_signal(barrier, inc=1, device_id={"clique": (me + d) % PIECES}, device_id_type=MESH)
-        return carry
-
-    lax.fori_loop(1, PIECES, body, 0)
+    for turn in TURNS:
+        pl.semaphore_signal(barrier, inc=1, device_id={"clique": turned(me, turn)}, device_id_type=MESH)
 
 
 def await_others():
@@ -376,9 +386,11 @@
     await_others()
 
 
-def send_pieces(me, source, target, sems):
-    def body(d, carry):
-        other = (me + d) % PIECES
+def send_pieces(me, source, target, sems, prepare=None):
+    for turn in TURNS:
+        other = turned(me, turn)
+        if prepare is not None:
+            prepare(other)
         pltpu.make_async_remote_copy(
             src_ref=source.at[other],
             dst_ref=target.at[me],
@@ -387,104 +399,6 @@
             device_id={"clique": other},
             device_id_type=MESH,
         ).start()
-        return carry
-
-    lax.fori_loop(1, PIECES, body, 0)
-
-
-def all_but_one(me, source, target, sems):
-    return pltpu.make_async_remote_copy(
-        src_ref=source.at[pl.ds(0, PIECES - 1)],
-        dst_ref=target.at[pl.ds(0, PIECES - 1)],
-        send_sem=sems.at[0],
-        recv_sem=sems.at[1],
-        device_id={"clique": (me + 1) % PIECES},
-        device_id_type=MESH,
-    )
-
-
-def gather_up(me, info, message, arrived, sums, sems):
-    enter(me)
-    send_pieces(me, message, arrived, sems)
-    arrived[me] = message[me]
-    all_but_one(me, message, arrived, sems).wait_recv()
-    sums[PIECES] = jnp.zeros((8, 128), F32)
-    for c in range(1, PIECES):
-        sums[c] = arrived[c] + sums[info[PREVIOUS + c]]
-    all_but_one(me, message, arrived, sems).wait_send()
-
-
-def sums_kernel(info, message, slots, arrived, sums, outgoing, incoming, sems, more_sems):
-    me = lax.axis_index("clique")
-    gather_up(me, info, message, arrived, sums, sems)
-
-    def body(p, carry):
-        for k in range(4):
-            outgoing[p, k] = sums[info[LAST + p * 4 + k]]
-        return carry
-
-    lax.fori_loop(0, PIECES, body, 0)
-    send_pieces(me, outgoing, incoming, more_sems)
-    incoming[me] = outgoing[me]
-    all_but_one(me, outgoing, incoming, more_sems).wait()
-    copy_slots(incoming, slots)
-
-
-def root_sums_kernel(info, message, old_slots, slots, arrived, sums, outgoing, incoming, sems, more_sems):
-    me = lax.axis_index("clique")
-    gather_up(me, info, message, arrived, sums, sems)
-    for k in range(4):
-        outgoing[k] = sums[info[LAST + k]]
-
-    @pl.when(me != 0)
-    def _():
-        copy = pltpu.make_async_remote_copy(
-            src_ref=outgoing,
-            dst_ref=incoming.at[me],
-            send_sem=more_sems.at[0],
-            recv_sem=more_sems.at[1],
-            device_id={"clique": 0},
-            device_id_type=MESH,
-        )
-        copy.start()
-        copy_slots(old_slots, slots)
-        copy.wait_send()
-
-    @pl.when(me == 0)
-    def _():
-        for k in range(4):
-            slots[0, k] = outgoing[k]
-        pltpu.make_async_remote_copy(
-            src_ref=incoming.at[pl.ds(1, PIECES - 1)],
-            dst_ref=incoming.at[pl.ds(1, PIECES - 1)],
-            send_sem=more_sems.at[0],
-            recv_sem=more_sems.at[1],
-            device_id={"clique": 1},
-            device_id_type=MESH,
-        ).wait_recv()
-
-        def body(piece, carry):
-            for k in range(4):
-                slots[piece, k] = incoming[piece, k]
-            return carry
-
-        lax.fori_loop(1, PIECES, body, 0)
-
-
-def send_slot(me, k, source, target, sems):
-    def body(d, carry):
-        other = (me + d) % PIECES
-        pltpu.make_async_remote_copy(
-            src_ref=source.at[other, k],
-            dst_ref=target.at[me, k],
-            send_sem=sems.at[0],
-            recv_sem=sems.at[1],
-            device_id={"clique": other},
-            device_id_type=MESH,
-        ).start()
-        return carry
-
-    lax.fori_loop(1, PIECES, body, 0)
 
 
 def part_of(me, count, source, target, sems):
@@ -498,46 +412,203 @@
     )
 
 
-def down_kernel(info, table, first, third, message, received, *scratch):
-    belief, margins, held, arrived, out_1, in_1, out_2, in_2 = scratch[:8]
-    work, sems = scratch[8:13], scratch[13:]
+def all_but_one(me, source, target, sems):
+    return part_of(me, PIECES - 1, source, target, sems)
+
+
+def gather_up(me, info, message, arrived, sums, sems):
+    enter(me)
+    send_pieces(me, message, arrived, sems)
+    arrived[me] = message[me]
+    sums[PIECES] = jnp.zeros((8, 128), F32)
+    all_but_one(me, message, arrived, sems).wait_recv()
+    for c in range(1, PIECES):
+        sums[c] = arrived[c] + sums[info[PREVIOUS + c]]
+    all_but_one(me, message, arrived, sems).wait_send()
+
+
+def sums_kernel(info, message, slots, arrived, sums, outgoing, sems, more_sems):
     me = lax.axis_index("clique")
+    gather_up(me, info, message, arrived, sums, sems)
+
+    def prepare(p):
+        for k in range(4):
+            outgoing[p, k] = sums[info[LAST + p * 4 + k]]
+
+    send_pieces(me, outgoing, slots, more_sems, prepare)
+    for k in range(4):
+        slots[me, k] = sums[info[LAST + me * 4 + k]]
+    all_but_one(me, outgoing, slots, more_sems).wait()
+
+
+def root_sums_kernel(info, message, old_slots, slots, arrived, sums, outgoing, sems, more_sems):
+    me = lax.axis_index("clique")
+    gather_up(me, info, message, arrived, sums, sems)
+
+    @pl.when(me != 0)
+    def _():
+        for k in range(4):
+            outgoing[k] = sums[info[LAST + k]]
+        copy = pltpu.make_async_remote_copy(
+            src_ref=outgoing,
+            dst_ref=slots.at[me],
+            send_sem=more_sems.at[0],
+            recv_sem=more_sems.at[1],
+            device_id={"clique": 0},
+            device_id_type=MESH,
+        )
+        copy.start()
+        copy_slots(old_slots, slots)
+        copy.wait_send()
+
+    @pl.when(me == 0)
+    def _():
+        for k in range(4):
+            slots[0, k] = sums[info[LAST + k]]
+        all_but_one(me, slots, slots, more_sems).wait_recv()
+
+
+def to_root(s, step, source, target, sems):
+    partner = 3 - s if step == 2 else s + 1 - 2 * (s % 2)
+    return partner, pltpu.make_async_remote_copy(
+        src_ref=source,
+        dst_ref=target,
+        send_sem=sems.at[0],
+        recv_sem=sems.at[1],
+        device_id={"subtree": partner},
+        device_id_type=MESH,
+    )
+
+
+def hop_kernel(step, sent, arrived, sems):
+    me, s = lax.axis_index("clique"), lax.axis_index("subtree")
+    partner, copy = to_root(s, step, sent, arrived, sems)
+    barrier = pltpu.get_barrier_semaphore()
+    receives = (me == 0) & inner_root(s)
+    sends = (me == 0) & (inner_root(s) == (step == 2))
+
+    @pl.when(receives)
+    def _():
+        pl.semaphore_signal(barrier, inc=1, device_id={"subtree": partner}, device_id_type=MESH)
+
+    @pl.when(sends)
+    def _():
+        pl.semaphore_wait(barrier, 1)
+        copy.start()
+
+    @pl.when(jnp.logical_not(receives))
+    def _():
+        for piece in range(PIECES):
+            arrived[piece] = jnp.zeros((8, 128), F32)
+
+    @pl.when(receives)
+    def _():
+        copy.wait_recv()
+
+    @pl.when(sends)
+    def _():
+        copy.wait_send()
+
+
+def send_slot(me, k, source, target, sems):
+    for turn in TURNS:
+        other = turned(me, turn)
+        pltpu.make_async_remote_copy(
+            src_ref=source.at[other, k],
+            dst_ref=target,
+            send_sem=sems.at[0],
+            recv_sem=sems.at[1],
+            device_id={"clique": other},
+            device_id_type=MESH,
+        ).start()
+
+
+def down_kernel(info, table, first, sent, message, received, last_root, *scratch):
+    belief, margins, held, arrived, from_root, third, out_1, in_1, out_2 = scratch[:9]
+    work, sems = scratch[9:14], scratch[14:]
+    me, s = lax.axis_index("clique"), lax.axis_index("subtree")
+    inner = inner_root(s)
+    sends, receives = (me == 0) & inner, (me == 0) & jnp.logical_not(inner)
+    partner, copy = to_root(s, 3, sent, third, sems[4])
+    barrier = pltpu.get_barrier_semaphore()
+
+    @pl.when(receives)
+    def _():
+        pl.semaphore_signal(barrier, inc=1, device_id={"subtree": partner}, device_id_type=MESH)
+
     announce(me)
 
-    def send_margins(pair):
+    @pl.when(sends)
+    def _():
+        pl.semaphore_wait(barrier, PIECES)
+        copy.start()
+
+    @pl.when(jnp.logical_not(sends))
+    def _():
+        pl.semaphore_wait(barrier, PIECES - 1)
+
+    def send_margins(pair, target):
         for k in (2, 1, 3, 0):
             MARGINS[k](belief, slot_put(margins, k), work)
-            send_slot(me, k, margins, arrived, pair)
+            send_slot(me, k, margins, target.at[k], pair)
         for k in range(4):
-            arrived[me, k] = margins[me, k]
+            target[k] = margins[me, k]
 
     @pl.when(me == 0)
     def _():
-        inner, slot = last_root_slot(info)
+        prepare_place(work[4])
+
+    @pl.when(receives)
+    def _():
+        copy.wait_recv()
 
         def body(piece, carry):
-            value = jnp.where(inner, first[piece], third[piece])
+            last_root[piece] = third[piece]
+            return carry
+
+        lax.fori_loop(0, PIECES, body, 0)
+
+    @pl.when(jnp.logical_not(receives))
+    def _():
+        def body(piece, carry):
+            last_root[piece] = first[piece]
+            return carry
+
+        lax.fori_loop(0, PIECES, body, 0)
+
+    @pl.when(me == 0)
+    def _():
+        slot = last_root_slot(info)
+
+        def body(piece, carry):
             for k in range(4):
-                held[piece, k] = jnp.where(slot == k, value, 0.0)
+                held[piece, k] = jnp.where(slot == k, last_root[piece], 0.0)
             return carry
 
         lax.fori_loop(0, PIECES, body, 0)
-        place_slots(table, belief, held, work[3:])
-
-    await_others()
-
-    @pl.when(me == 0)
-    def _():
-        send_margins(sems[0])
+        place_slots(table, belief, held, work[3:], prepared=True)
+        send_margins(sems[0], from_root)
 
     @pl.when(me != 0)
     def _():
-        part_of(me, 1, margins, arrived, sems[0]).wait_recv()
-
-    for c in range(PIECES):
-        out_1[c] = arrived[0, info[SOURCE + c] % 4]
-    send_pieces(me, out_1, in_1, sems[1])
-    in_1[me] = out_1[me]
+        prepare_place(work[4])
+        pltpu.make_async_remote_copy(
+            src_ref=from_root,
+            dst_ref=from_root,
+            send_sem=sems[0].at[0],
+            recv_sem=sems[0].at[1],
+            device_id={"clique": 0},
+            device_id_type=MESH,
+        ).wait_recv()
+
+    for k in range(4):
+        arrived[0, k] = from_root[k]
+
+    def prepare_1(c):
+        out_1[c] = from_root[info[SOURCE + c] % 4]
+
+    send_pieces(me, out_1, in_1, sems[1], prepare_1)
+    in_1[me] = from_root[info[SOURCE + me] % 4]
     all_but_one(me, out_1, in_1, sems[1]).wait()
 
     @pl.when(me != 0)
@@ -551,25 +622,20 @@
             return carry
 
         lax.fori_loop(0, PIECES, body, 0)
-        place_slots(table, belief, held, work[3:])
-        send_margins(sems[2])
+        place_slots(table, belief, held, work[3:], prepared=True)
+        send_margins(sems[2], arrived.at[me])
         part_of(me, PIECES - 2, margins, arrived, sems[2]).wait_recv()
 
     @pl.when(me == 0)
     def _():
         part_of(me, PIECES - 1, margins, arrived, sems[2]).wait_recv()
 
-    for c in range(PIECES):
+    def prepare_2(c):
         out_2[c] = arrived[info[SOURCE + c] // 4, info[SOURCE + c] % 4]
-    send_pieces(me, out_2, in_2, sems[3])
-    in_2[me] = out_2[me]
-    all_but_one(me, out_2, in_2, sems[3]).wait()
-
-    def body(piece, carry):
-        received[piece] = in_2[piece]
-        return carry
-
-    lax.fori_loop(0, PIECES, body, 0)
+
+    send_pieces(me, out_2, received, sems[3], prepare_2)
+    received[me] = arrived[info[SOURCE + me] // 4, info[SOURCE + me] % 4]
+    all_but_one(me, out_2, received, sems[3]).wait()
 
     @pl.when(me == 0)
     def _():
@@ -578,6 +644,10 @@
     @pl.when(me != 0)
     def _():
         part_of(me, PIECES - 1, margins, arrived, sems[2]).wait_send()
+
+    @pl.when(sends)
+    def _():
+        copy.wait_send()
 
 
 MESSAGE = jax.ShapeDtypeStruct((PIECES, 8, 128), F32)
@@ -629,7 +699,7 @@
         [S_SPEC, V_SPEC],
         SLOTS,
         V_SPEC,
-        [HELD_MESSAGE, HELD_SUMS, HELD_SLOTS, HELD_SLOTS, PAIR_SEMS, PAIR_SEMS],
+        [HELD_MESSAGE, HELD_SUMS, HELD_SLOTS, PAIR_SEMS, PAIR_SEMS],
         collective=0,
     )(info, message)
     message = call(
@@ -641,14 +711,25 @@
         [S_SPEC] + [V_SPEC] * 2,
         SLOTS,
         V_SPEC,
-        [HELD_MESSAGE, HELD_SUMS, HELD_PIECE, HELD_SLOTS, PAIR_SEMS, PAIR_SEMS],
+        [HELD_MESSAGE, HELD_SUMS, HELD_PIECE, PAIR_SEMS, PAIR_SEMS],
         collective=1,
     )(info, message, slots)
-    axes = ("clique", "subtree")
+
+    def hop(step, sent):
+        return call(
+            functools.partial(hop_kernel, step),
+            f"hop_{step}",
+            [V_SPEC],
+            MESSAGE,
+            V_SPEC,
+            [PAIR_SEMS],
+            collective=2 + step,
+        )(sent)
+
     sent, table = call(
         chain_first_kernel, "chain_1", [S_SPEC] + [V_SPEC] * 2, (MESSAGE, TABLE), (V_SPEC, V_SPEC), WORK
     )(info, table, slots)
-    first = lax.ppermute(sent, axes, ((3, 2), (0, 1)))
+    first = hop(1, sent)
     sent = call(
         functools.partial(chain_kernel, 2),
         "chain_2",
@@ -657,7 +738,7 @@
         V_SPEC,
         [HELD_TABLE] + WORK,
     )(info, table, first)
-    second = lax.ppermute(sent, axes, ((2, 1), (1, 2)))
+    second = hop(2, sent)
     sent, table = call(
         functools.partial(chain_kernel, 3),
         "chain_3",
@@ -666,24 +747,23 @@
         (V_SPEC, V_SPEC),
         WORK,
     )(info, table, second)
-    third = lax.ppermute(sent, axes, ((1, 0), (2, 3)))
-    received = call(
+    received, last_root = call(
         down_kernel,
         "down",
         [S_SPEC] + [V_SPEC] * 4,
-        MESSAGE,
-        V_SPEC,
-        [HELD_TABLE] + [HELD_SLOTS] * 3 + [HELD_MESSAGE] * 4 + WORK + [PAIR_SEMS] * 4,
+        (MESSAGE, MESSAGE),
+        (V_SPEC, V_SPEC),
+        [HELD_TABLE] + [HELD_SLOTS] * 3 + [HELD_PIECE] + [HELD_MESSAGE] * 4 + WORK + [PAIR_SEMS] * 5,
         collective=2,
-    )(info, table, first, third, message)
+    )(info, table, first, sent, message)
     out = call(
         final_kernel,
         "final",
-        [S_SPEC] + [V_SPEC] * 5,
+        [S_SPEC] + [V_SPEC] * 4,
         TABLE,
         ANY_SPEC,
         [HELD_TABLE, HELD_MESSAGE] + PLACE_TOOLS + [pltpu.SemaphoreType.DMA((4,))],
-    )(info, table, first, third, received, message)
+    )(info, table, last_root, received, message)
     return out.reshape(1, 1, 1024, 1024)
 
 

time: 124 us -> 113 us (0.911)
  Pallas kernels: 120 us -> 112 us
  starting transfers between devices: 2.01 us -> 0 us
    pallas_call x1, Pallas kernels: 4.52 us -> 2.37 us  [per_device(): call(chain_first_kernel, 'chain_1', [S_SPEC] + [V_SPEC] * 2, (MESSAGE, TA...]
    ppermute x3 -> x0, starting transfers between devices: 2.01 us -> none  [the longest x1 0.67 us: per_device(): third = lax.ppermute(sent, axes, ((1, 0), (2, 3)))]
    pallas_call x1, Pallas kernels: 3.65 us -> 2.24 us  [per_device(): call(functools.partial(chain_kernel, 2), 'chain_2', [S_SPEC] + [V_SPEC] *...]
    pallas_call x1, Pallas kernels: 3.66 us -> 2.24 us  [per_device(): call(functools.partial(chain_kernel, 3), 'chain_3', [S_SPEC] + [V_SPEC] *...]
    pallas_call x1, Pallas kernels: 10.3 us -> 9 us  [per_device(): call(root_sums_kernel, 'root_sums', [S_SPEC] + [V_SPEC] * 2, SLOTS, V_SPE...]
    pallas_call x1, Pallas kernels: 22.1 us -> 20.8 us  [per_device(): call(sums_kernel, 'sums', [S_SPEC, V_SPEC], SLOTS, V_SPEC, [HELD_MESSAGE,...]
    pallas_call x2 -> x4, Pallas kernels: 66.5 us -> 65.9 us  [the longest x1 62.5 us: per_device(): call(down_kernel, 'down', [S_SPEC] + [V_SPEC] * 4, (MESSAGE, MESSAGE), (V...]
  transfers between devices with their start and end apart: 3 -> 0, of which waited for: 0 -> 0; matrix products, arithmetic and copies ran while one was open for 0% -> 0% of each run, Pallas kernels for 0% -> 0%
where the time goes in v4:
time: 113 us
  Pallas kernels  112 us (99%)
    pallas_call x1, Pallas kernels, per_device(): call(down_kernel, 'down', [S_SPEC] + [V_SPEC] * 4, (MESSAGE, MESSAGE), (V...  62.5 us
    pallas_call x1, Pallas kernels, per_device(): call(sums_kernel, 'sums', [S_SPEC, V_SPEC], SLOTS, V_SPEC, [HELD_MESSAGE,...  20.8 us
    pallas_call x1, Pallas kernels, per_device(): call(root_sums_kernel, 'root_sums', [S_SPEC] + [V_SPEC] * 2, SLOTS, V_SPE...  9 us
    pallas_call x1, Pallas kernels, per_device(): call(first_kernel, 'first', [ANY_SPEC] * 2, (MESSAGE, jax.ShapeDtypeStruc...  5.16 us
    pallas_call x1, Pallas kernels, per_device(): call(up_kernel, 'up', [S_SPEC] + [V_SPEC] * 2, MESSAGE, V_SPEC, [HELD_TAB...  4.5 us
    pallas_call x1, Pallas kernels, per_device(): call(final_kernel, 'final', [S_SPEC] + [V_SPEC] * 4, TABLE, ANY_SPEC, [HE...  3.12 us
    pallas_call x1, Pallas kernels, per_device(): call(chain_first_kernel, 'chain_1', [S_SPEC] + [V_SPEC] * 2, (MESSAGE, TA...  2.37 us

profile of v4, /device:TPU:1, one launch (start us, length us, event | category | flops | bytes accessed | tf_op | source)
XLA Modules:
  0.0 113.3 jit_solution(17772376648080747058)
XLA Ops:
  0.0 0.0 copy-start
  0.0 0.9 pad_add_fusion.trees_in
  0.9 5.2 %first.1 = (f32[32,8,128]{2,1,0:T(8,128)S(1)}, s32[256]{0:T(256)S(1)}) custom-call(s32[9,32]{1,0:T(8,128)S(1)} %pad_add_fusion.trees_in, f32[1024,1024]{1,0:T(8,128)} %bitcast.2), custom_call_target="tpu_custom_call" | custom-call | tf_op jit(solution)/shard_map/first/pallas_call | solution.py:685
  6.0 20.8 %sums.1.slots.old_slots = f32[32,4,8,128]{3,2,1,0:T(8,128)S(1)} custom-call(s32[256]{0:T(256)S(1)} %get-tuple-element.13.info, f32[32,8,128]{2,1,0:T(8,128)S(1)} %get-tuple-element.14.message), custom_call_target="tpu_custom_call" | custom-call | tf_op jit(solution)/shard_map/sums/pallas_call | solution.py:696
  26.9 0.0 copy-done
  26.9 4.5 %up.1.message = f32[32,8,128]{2,1,0:T(8,128)S(1)} custom-call(s32[256]{0:T(256)S(1)} %get-tuple-element.13.info, f32[1024,1024]{1,0:T(8,128)S(1)} %bitcast.3, f32[32,4,8,128]{3,2,1,0:T(8,128)S(1)} %sums.1.slots.old_slots), custom_call_target="tpu_custom_call" | custom-call | tf_op jit(solution)/shard_map/up/pallas_call | solution.py:705
  31.4 9.0 %root_sums.1.slots = f32[32,4,8,128]{3,2,1,0:T(8,128)S(1)} custom-call(s32[256]{0:T(256)S(1)} %get-tuple-element.13.info, f32[32,8,128]{2,1,0:T(8,128)S(1)} %up.1.message, f32[32,4,8,128]{3,2,1,0:T(8,128)S(1)} %sums.1.slots.old_slots), custom_call_target="tpu_custom_call" | custom-call | tf_op jit(solution)/shard_map/root_sums/pallas_call | solution.py:708
  40.4 2.4 %chain_1.1 = (f32[32,8,128]{2,1,0:T(8,128)S(1)}, f32[1024,1024]{1,0:T(8,128)S(1)}) custom-call(s32[256]{0:T(256)S(1)} %get-tuple-element.13.info, f32[1024,1024]{1,0:T(8,128)S(1)} %bitcast.4, f32[32,4,8,128]{3,2,1,0:T(8,128)S(1)} %root_sums.1.slots), custom_call_target="tpu_custom_call" | custom-call | tf_op jit(solution)/shard_map/chain_1/pallas_call | solution.py:729
  42.8 0.1 hop_1.1.arrived.first
  42.9 2.2 %chain_2.1.sent = f32[32,8,128]{2,1,0:T(8,128)S(1)} custom-call(s32[256]{0:T(256)S(1)} %get-tuple-element.13.info, f32[1024,1024]{1,0:T(8,128)S(1)} %get-tuple-element.15.table, f32[32,8,128]{2,1,0:T(8,128)S(1)} %hop_1.1.arrived.first), custom_call_target="tpu_custom_call" | custom-call | tf_op jit(solution)/shard_map/chain_2/pallas_call | solution.py:733
  45.2 0.1 hop_2.1.arrived
  45.3 2.2 %chain_3.1 = (f32[32,8,128]{2,1,0:T(8,128)S(1)}, f32[1024,1024]{1,0:T(8,128)S(1)}) custom-call(s32[256]{0:T(256)S(1)} %get-tuple-element.13.info, f32[1024,1024]{1,0:T(8,128)S(1)} %get-tuple-element.15.table, f32[32,8,128]{2,1,0:T(8,128)S(1)} %hop_2.1.arrived), custom_call_target="tpu_custom_call" | custom-call | tf_op jit(solution)/shard_map/chain_3/pallas_call | solution.py:742
  47.5 62.5 %down.1 = (f32[32,8,128]{2,1,0:T(8,128)S(1)}, f32[32,8,128]{2,1,0:T(8,128)S(1)}) custom-call(s32[256]{0:T(256)S(1)} %get-tuple-element.13.info, f32[1024,1024]{1,0:T(8,128)S(1)} %get-tuple-element.17.table, f32[32,8,128]{2,1,0:T(8,128)S(1)} %hop_1.1.arrived.first, f32[32,8,128]{2,1,0:T(8,128)S(1)} %get-tuple-element.18.sent, f32[32,8,128]{2,1,0:T(8,128)S(1)} %up.1.message), custom_call_target="tpu_custom_call" | custom-call | tf_op jit(solution)/shard_map/down/pallas_call | solution.py:750
  110.0 3.1 %final.1 = f32[1024,1024]{1,0:T(8,128)} custom-call(s32[256]{0:T(256)S(1)} %get-tuple-element.13.info, f32[1024,1024]{1,0:T(8,128)S(1)} %get-tuple-element.17.table, f32[32,8,128]{2,1,0:T(8,128)S(1)} %get-tuple-element.19.last_root, f32[32,8,128]{2,1,0:T(8,128)S(1)} %get-tuple-element.20.received, f32[32,8,128]{2,1,0:T(8,128)S(1)} %up.1.message), custom_call_target="tpu_custom_call" | custom-call | tf_op jit(solution)/shard_map/final/pallas_call | solution.py:759
Async XLA Ops:
  0.0 26.9 %copy-start = (f32[1,1,1024,1024]{3,2,1,0:T(8,128)S(1)}, f32[1,1,1024,1024]{3,2,1,0:T(8,128)}, u32[]{:S(2)}) copy-start(f32[1,1,1024,1024]{3,2,1,0:T(8,128)} %param.4) | copy-start | bytes 12582916

commit v5 on v4

--- a/solution.py
+++ b/solution.py
@@ -105,12 +105,10 @@
     lax.fori_loop(0, 4, body, 0)
 
 
-def place_slots(source, target, slots, tools, after=None, prepared=False):
+def place_slots(source, target, slots, tools, after=None):
     def readers(k):
         return lambda piece: slots[piece, k], lambda piece, s: slots[piece, k, pl.ds(s, 1), :]
 
-    if not prepared:
-        prepare_place(tools[1])
     place(source, target, {k: readers(k) for k in range(4)}, tools, after)
 
 
@@ -120,8 +118,6 @@
         @pl.when(axis == k)
         def _(k=k):
             readers = (lambda piece: message[piece], lambda piece, s: message[piece, pl.ds(s, 1), :])
-            if k == 3:
-                prepare_place(tools[1])
             place(source, target, {k: readers}, tools, after)
 
 
@@ -132,7 +128,11 @@
     )
 
 
-def margin_0(table, put, work):
+def margin_0(table, put, work, before=None):
+    if before is not None:
+        for n in range(CHUNKS):
+            before(n)
+
     def body(i, carry):
         for t in range(8):
             parts = [tile(table, a0, i, t) for a0 in range(32)]
@@ -150,7 +150,18 @@
     return vec
 
 
-def margin_1(table, put, work):
+def by_blocks(body, before):
+    def block(n, carry):
+        if before is not None:
+            before(n)
+        for a0 in range(4):
+            body(n * 4 + a0, carry)
+        return carry
+
+    lax.fori_loop(0, 8, block, 0)
+
+
+def margin_1(table, put, work, before=None):
     def body(a0, carry):
         for t in range(8):
             parts = [tile(table, a0, i, t) for i in range(4)]
@@ -159,75 +170,64 @@
             put((a0 // 8) * 8 + t, 1, a0 % 8, (top + jnp.log(total))[0:1])
         return carry
 
-    lax.fori_loop(0, 32, body, 0)
-
-
-def margin_2(table, put, work):
-    totals, tops = work[0], work[1]
-
-    def largest(a0, carry):
-        for i in range(4):
-            at = pl.ds(pl.multiple_of((a0 * 4 + i) * 8, 8), 8)
-            totals[at, :] = tree([tile(table, a0, i, t) for t in range(8)], jnp.maximum)
-        return carry
-
-    lax.fori_loop(0, 32, largest, 0, unroll=4)
-
-    def groups(n, carry):
-        ats = [pl.ds(pl.multiple_of((n * 32 + m) * 8, 8), 8) for m in range(32)]
-        parts = [totals[at, :] for at in ats]
-        for shift in (64, 32):
-            moved = [pltpu.roll(part, shift, 1) for part in parts]
-            parts = [jnp.maximum(part, other) for part, other in zip(parts, moved)]
-        for at, part in zip(ats, parts):
-            tops[at, :] = part
-        return carry
-
-    lax.fori_loop(0, 4, groups, 0)
-
-    def sums(a0, carry):
-        for i in range(4):
-            at = pl.ds(pl.multiple_of((a0 * 4 + i) * 8, 8), 8)
-            top = tops[at, :]
-            totals[at, :] = tree([jnp.exp(tile(table, a0, i, t) - top) for t in range(8)], jnp.add)
-        return carry
-
-    lax.fori_loop(0, 32, sums, 0, unroll=2)
-
-    def pack(part, carry):
-        packed = []
-        for s in range(8):
-            start = (part * 8 + s) * 32
-            total = [totals[pl.ds(start + q, 8, stride=4), :] for q in range(4)]
-            top = pick([tops[pl.ds(start + q, 8, stride=4), :] for q in range(4)])
-            turned = [pick([total[(g + r) % 4] for g in range(4)]) for r in range(4)]
-            packed.append((top, [turned[0]] + [pltpu.roll(turned[r], 32 * r, 1) for r in range(1, 4)]))
-        for s, (top, turned) in enumerate(packed):
-            put(part * 8, 8, s, top + jnp.log((turned[0] + turned[1]) + (turned[2] + turned[3])))
-        return carry
-
-    lax.fori_loop(0, 4, pack, 0)
-
-
-def margin_3(table, put, work):
-    flat, across = work[0], work[2]
-
-    def body(block, carry):
-        for t in range(8):
-            turned = table[pl.ds(pl.multiple_of(block * 128, 128), 128), 128 * t : 128 * (t + 1)].T
-            for g in range(4):
-                parts = [turned[32 * g + 8 * m : 32 * g + 8 * (m + 1)] for m in range(4)]
-                top = over_rows(tree(parts, jnp.maximum), jnp.maximum)
-                total = over_rows(tree([jnp.exp(part - top) for part in parts], jnp.add), jnp.add)
-                across[block, 4 * t + g : 4 * t + g + 1, :] = (top + jnp.log(total))[0:1]
-        return carry
-
-    lax.fori_loop(0, 8, body, 0, unroll=2)
+    by_blocks(body, before)
+
+
+def put_turned(across, flat, put):
     for block in range(8):
         part = across[block]
         flat[128 * block : 128 * (block + 1), :] = jnp.concatenate([part] * 4, axis=0).T
     for a0 in range(32):
         put((a0 // 8) * 8, 8, a0 % 8, pick([flat[pl.ds(a0 * 32 + q, 8, stride=4), :] for q in range(4)]))
+
+
+def turned_margins(table, put_2, put_3, work, before=None):
+    flat, across_2, across_3, kept = work[:4]
+
+    def body(block, carry):
+        if before is not None:
+            before(block)
+        tops = None
+        for t in range(8):
+            turned = table[pl.ds(pl.multiple_of(block * 128, 128), 128), 128 * t : 128 * (t + 1)].T
+            tiles = [[turned[32 * g + 8 * m : 32 * g + 8 * (m + 1)] for m in range(4)] for g in range(4)]
+            if put_3 is not None:
+                for g in range(4):
+                    top = over_rows(tree(tiles[g], jnp.maximum), jnp.maximum)
+                    total = over_rows(tree([jnp.exp(part - top) for part in tiles[g]], jnp.add), jnp.add)
+                    across_3[block, 4 * t + g : 4 * t + g + 1, :] = (top + jnp.log(total))[0:1]
+            if put_2 is not None:
+                kept[block, t] = turned
+                here = [tree([tiles[g][m] for g in range(4)], jnp.maximum) for m in range(4)]
+                tops = here if tops is None else [jnp.maximum(a, b) for a, b in zip(tops, here)]
+        if put_2 is not None:
+            totals = None
+            for t in range(8):
+                here = [
+                    tree(
+                        [jnp.exp(kept[block, t, 32 * g + 8 * m : 32 * g + 8 * (m + 1), :] - tops[m]) for g in range(4)],
+                        jnp.add,
+                    )
+                    for m in range(4)
+                ]
+                totals = here if totals is None else [a + b for a, b in zip(totals, here)]
+            for m in range(4):
+                across_2[block, 8 * m : 8 * (m + 1), :] = tops[m] + jnp.log(totals[m])
+        return carry
+
+    lax.fori_loop(0, 8, body, 0, unroll=4)
+    if put_2 is not None:
+        put_turned(across_2, flat, put_2)
+    if put_3 is not None:
+        put_turned(across_3, flat, put_3)
+
+
+def margin_2(table, put, work, before=None):
+    turned_margins(table, put, None, work, before)
+
+
+def margin_3(table, put, work, before=None):
+    turned_margins(table, None, put, work, before)
 
 
 MARGINS = (margin_0, margin_1, margin_2, margin_3)
@@ -257,12 +257,12 @@
     return put
 
 
-def chosen_margin(table, axis, message, work):
+def chosen_margin(table, axis, message, work, before=None):
     for k in range(4):
 
         @pl.when(axis == k)
         def _(k=k):
-            MARGINS[k](table, message_put(message), work)
+            MARGINS[k](table, message_put(message), work, before)
 
 
 def copy_slots(source, target):
@@ -277,20 +277,20 @@
 PREVIOUS, LAST, SOURCE, OWN_DROP, CHAIN_AXIS, CHAIN_SLOT, INFO = 0, 32, 160, 192, 192, 196, 256
 
 
-def first_kernel(trees_in, potentials, message, info, table, trees, *rest):
-    work, load_sems, sems = rest[:5], rest[5], rest[6]
+def first_kernel(trees_in, potentials, message, info, hot, table, trees, *rest):
+    work, load_sems, sems = rest[:4], rest[4], rest[5]
     me, s = lax.axis_index("clique"), lax.axis_index("subtree")
     size = 1024 // CHUNKS
-    loads = [
-        pltpu.make_async_copy(
-            potentials.at[pl.ds(size * n, size)], table.at[pl.ds(size * n, size)], load_sems.at[n]
-        )
-        for n in range(CHUNKS)
-    ]
+
+    def load(n):
+        at = pl.ds(pl.multiple_of(size * n, size), size)
+        return pltpu.make_async_copy(potentials.at[at], table.at[at], load_sems.at[n])
+
     small = pltpu.make_async_copy(trees_in, trees, sems)
     small.start()
-    for copy in loads:
-        copy.start()
+    for n in range(CHUNKS):
+        load(n).start()
+    prepare_place(hot)
     for n in range(128):
         info[LAST + n] = PIECES
     small.wait()
@@ -313,23 +313,21 @@
         active = (me == 0) & (((s == 1) | (s == 2)) == (step > 1))
         info[CHAIN_AXIS + step] = jnp.where(active, jnp.where(s == sender, to_next, to_previous), 4)
         info[CHAIN_SLOT + step] = jnp.where(s == receiver, to_next, to_previous)
-    for copy in loads:
-        copy.wait()
-    chosen_margin(table, own, message, work)
-
-
-def up_kernel(info, table, slots, message, placed, *work):
-    place_slots(table, placed, slots, work[3:])
+    chosen_margin(table, own, message, work, lambda n: load(n).wait())
+
+
+def up_kernel(info, hot, table, slots, message, placed, *work):
+    place_slots(table, placed, slots, (work[4], hot))
     chosen_margin(placed, info[OWN_DROP], message, work)
 
 
-def chain_first_kernel(info, table, slots, message, placed, *work):
-    place_slots(table, placed, slots, work[3:])
+def chain_first_kernel(info, hot, table, slots, message, placed, *work):
+    place_slots(table, placed, slots, (work[4], hot))
     chosen_margin(placed, info[CHAIN_AXIS + 1], message, work)
 
 
-def chain_kernel(step, info, table, arrived, message, placed, *work):
-    place_message(table, placed, arrived, info[CHAIN_SLOT + step - 1], work[3:])
+def chain_kernel(step, info, hot, table, arrived, message, placed, *work):
+    place_message(table, placed, arrived, info[CHAIN_SLOT + step - 1], (work[4], hot))
     chosen_margin(placed, info[CHAIN_AXIS + step], message, work)
 
 
@@ -342,7 +340,7 @@
     return jnp.where(inner, info[CHAIN_SLOT + 1], info[CHAIN_SLOT + 3])
 
 
-def final_kernel(info, table, last_root, received, message, out, belief, held, left, hot, sems):
+def final_kernel(info, hot, table, last_root, received, message, out, belief, held, left, sems):
     below = lax.axis_index("clique") != 0
     top = jnp.max(tree([received[piece] for piece in range(PIECES)], jnp.maximum))
     total = tree([jnp.exp(received[piece] - top) for piece in range(PIECES)], jnp.add)
@@ -510,11 +508,11 @@
         copy.wait_send()
 
 
-def send_slot(me, k, source, target, sems):
+def send_slots(me, start, source, target, sems):
     for turn in TURNS:
         other = turned(me, turn)
         pltpu.make_async_remote_copy(
-            src_ref=source.at[other, k],
+            src_ref=source.at[other, pl.ds(start, 1)],
             dst_ref=target,
             send_sem=sems.at[0],
             recv_sem=sems.at[1],
@@ -523,9 +521,10 @@
         ).start()
 
 
-def down_kernel(info, table, first, sent, message, received, last_root, *scratch):
+def down_kernel(info, hot, table, first, sent, message, received, last_root, *scratch):
     belief, margins, held, arrived, from_root, third, out_1, in_1, out_2 = scratch[:9]
     work, sems = scratch[9:14], scratch[14:]
+    tools = (work[4], hot)
     me, s = lax.axis_index("clique"), lax.axis_index("subtree")
     inner = inner_root(s)
     sends, receives = (me == 0) & inner, (me == 0) & jnp.logical_not(inner)
@@ -547,16 +546,16 @@
     def _():
         pl.semaphore_wait(barrier, PIECES - 1)
 
-    def send_margins(pair, target):
-        for k in (2, 1, 3, 0):
-            MARGINS[k](belief, slot_put(margins, k), work)
-            send_slot(me, k, margins, target.at[k], pair)
+    def send_margins(pair, target, order):
+        for group in order:
+            if len(group) == 2:
+                turned_margins(belief, slot_put(margins, 2), slot_put(margins, 3), work)
+            else:
+                MARGINS[group[0]](belief, slot_put(margins, group[0]), work)
+            for k in group:
+                send_slots(me, k, margins, target.at[pl.ds(k, 1)], pair)
         for k in range(4):
             target[k] = margins[me, k]
-
-    @pl.when(me == 0)
-    def _():
-        prepare_place(work[4])
 
     @pl.when(receives)
     def _():
@@ -586,12 +585,11 @@
             return carry
 
         lax.fori_loop(0, PIECES, body, 0)
-        place_slots(table, belief, held, work[3:], prepared=True)
-        send_margins(sems[0], from_root)
+        place_slots(table, belief, held, tools)
+        send_margins(sems[0], from_root, ((2, 3), (1,), (0,)))
 
     @pl.when(me != 0)
     def _():
-        prepare_place(work[4])
         pltpu.make_async_remote_copy(
             src_ref=from_root,
             dst_ref=from_root,
@@ -622,8 +620,8 @@
             return carry
 
         lax.fori_loop(0, PIECES, body, 0)
-        place_slots(table, belief, held, work[3:], prepared=True)
-        send_margins(sems[2], arrived.at[me])
+        place_slots(table, belief, held, tools)
+        send_margins(sems[2], arrived.at[me], ((0,), (1,), (2, 3)))
         part_of(me, PIECES - 2, margins, arrived, sems[2]).wait_recv()
 
     @pl.when(me == 0)
@@ -661,8 +659,9 @@
 HELD_SLOTS = VMEM((PIECES, 4, 8, 128), F32)
 HELD_PIECE = VMEM((4, 8, 128), F32)
 HELD_TABLE = VMEM((1024, 1024), F32)
-PLACE_TOOLS = [VMEM((256, 256), jnp.bfloat16), VMEM((256, 1024), jnp.bfloat16)]
-WORK = [VMEM((1024, 128), F32), VMEM((1024, 128), F32), VMEM((8, 32, 128), F32)] + PLACE_TOOLS
+LEFT = VMEM((256, 256), jnp.bfloat16)
+HOT = jax.ShapeDtypeStruct((256, 1024), jnp.bfloat16)
+WORK = [VMEM((1024, 128), F32), VMEM((8, 32, 128), F32), VMEM((8, 32, 128), F32), VMEM((8, 8, 128, 128), F32), LEFT]
 PAIR_SEMS = pltpu.SemaphoreType.DMA((2,))
 
 
@@ -682,14 +681,14 @@
 def per_device(potentials, parent, child_drop, parent_drop):
     table = potentials.reshape(1024, 1024)
     trees = jnp.concatenate([child_drop, parent_drop, parent])
-    message, info = call(
+    message, info, hot = call(
         first_kernel,
         "first",
         [ANY_SPEC] * 2,
-        (MESSAGE, jax.ShapeDtypeStruct((INFO,), jnp.int32)),
-        (V_SPEC, S_SPEC),
+        (MESSAGE, jax.ShapeDtypeStruct((INFO,), jnp.int32), HOT),
+        (V_SPEC, S_SPEC, V_SPEC),
         [HELD_TABLE, SMEM((9, 32), jnp.int32)]
-        + WORK
+        + WORK[:4]
         + [pltpu.SemaphoreType.DMA((CHUNKS,)), pltpu.SemaphoreType.DMA],
         limit=53,
     )(trees, table)
@@ -703,8 +702,8 @@
         collective=0,
     )(info, message)
     message = call(
-        up_kernel, "up", [S_SPEC] + [V_SPEC] * 2, MESSAGE, V_SPEC, [HELD_TABLE] + WORK
-    )(info, table, slots)
+        up_kernel, "up", [S_SPEC] + [V_SPEC] * 3, MESSAGE, V_SPEC, [HELD_TABLE] + WORK
+    )(info, hot, table, slots)
     slots = call(
         root_sums_kernel,
         "root_sums",
@@ -727,43 +726,43 @@
         )(sent)
 
     sent, table = call(
-        chain_first_kernel, "chain_1", [S_SPEC] + [V_SPEC] * 2, (MESSAGE, TABLE), (V_SPEC, V_SPEC), WORK
-    )(info, table, slots)
+        chain_first_kernel, "chain_1", [S_SPEC] + [V_SPEC] * 3, (MESSAGE, TABLE), (V_SPEC, V_SPEC), WORK
+    )(info, hot, table, slots)
     first = hop(1, sent)
     sent = call(
         functools.partial(chain_kernel, 2),
         "chain_2",
-        [S_SPEC] + [V_SPEC] * 2,
+        [S_SPEC] + [V_SPEC] * 3,
         MESSAGE,
         V_SPEC,
         [HELD_TABLE] + WORK,
-    )(info, table, first)
+    )(info, hot, table, first)
     second = hop(2, sent)
     sent, table = call(
         functools.partial(chain_kernel, 3),
         "chain_3",
-        [S_SPEC] + [V_SPEC] * 2,
+        [S_SPEC] + [V_SPEC] * 3,
         (MESSAGE, TABLE),
         (V_SPEC, V_SPEC),
         WORK,
-    )(info, table, second)
+    )(info, hot, table, second)
     received, last_root = call(
         down_kernel,
         "down",
-        [S_SPEC] + [V_SPEC] * 4,
+        [S_SPEC] + [V_SPEC] * 5,
         (MESSAGE, MESSAGE),
         (V_SPEC, V_SPEC),
         [HELD_TABLE] + [HELD_SLOTS] * 3 + [HELD_PIECE] + [HELD_MESSAGE] * 4 + WORK + [PAIR_SEMS] * 5,
         collective=2,
-    )(info, table, first, sent, message)
+    )(info, hot, table, first, sent, message)
     out = call(
         final_kernel,
         "final",
-        [S_SPEC] + [V_SPEC] * 4,
+        [S_SPEC] + [V_SPEC] * 5,
         TABLE,
         ANY_SPEC,
-        [HELD_TABLE, HELD_MESSAGE] + PLACE_TOOLS + [pltpu.SemaphoreType.DMA((4,))],
-    )(info, table, last_root, received, message)
+        [HELD_TABLE, HELD_MESSAGE, LEFT, pltpu.SemaphoreType.DMA((4,))],
+    )(info, hot, table, last_root, received, message)
     return out.reshape(1, 1, 1024, 1024)
 
 

time: 113 us -> 107 us (0.947)
  Pallas kernels: 112 us -> 105 us
    pallas_call x4, Pallas kernels: 72.5 us -> 67.1 us  [the longest x1 57.7 us: per_device(): call(down_kernel, 'down', [S_SPEC] + [V_SPEC] * 5, (MESSAGE, MESSAGE), (V...]
where the time goes in v5:
time: 107 us; the launch traced here: 106 us
  Pallas kernels  105 us (98%)
    pallas_call x1, Pallas kernels, per_device(): call(down_kernel, 'down', [S_SPEC] + [V_SPEC] * 5, (MESSAGE, MESSAGE), (V...  57.7 us
    pallas_call x1, Pallas kernels, per_device(): call(sums_kernel, 'sums', [S_SPEC, V_SPEC], SLOTS, V_SPEC, [HELD_MESSAGE,...  20.6 us
    pallas_call x1, Pallas kernels, per_device(): call(root_sums_kernel, 'root_sums', [S_SPEC] + [V_SPEC] * 2, SLOTS, V_SPE...  9.7 us
    pallas_call x1, Pallas kernels, per_device(): call(first_kernel, 'first', [ANY_SPEC] * 2, (MESSAGE, jax.ShapeDtypeStruc...  4.45 us
    pallas_call x1, Pallas kernels, per_device(): call(up_kernel, 'up', [S_SPEC] + [V_SPEC] * 3, MESSAGE, V_SPEC, [HELD_TAB...  3.98 us
    pallas_call x1, Pallas kernels, per_device(): call(final_kernel, 'final', [S_SPEC] + [V_SPEC] * 5, TABLE, ANY_SPEC, [HE...  3.12 us
    pallas_call x1, Pallas kernels, per_device(): call(chain_first_kernel, 'chain_1', [S_SPEC] + [V_SPEC] * 3, (MESSAGE, TA...  2.37 us

profile of v5, /device:TPU:1, one launch (start us, length us, event | category | flops | bytes accessed | tf_op | source)
XLA Modules:
  0.0 106.4 jit_solution(15750776484773142785)
XLA Ops:
  0.0 0.0 copy-start
  0.0 0.9 pad_add_fusion.trees_in
  0.9 4.5 %first.1 = (f32[32,8,128]{2,1,0:T(8,128)S(1)}, s32[256]{0:T(256)S(1)}, bf16[256,1024]{1,0:T(8,128)(2,1)S(1)}) custom-call(s32[9,32]{1,0:T(8,128)S(1)} %pad_add_fusion.trees_in, f32[1024,1024]{1,0:T(8,128)} %bitcast.2), custom_call_target="tpu_custom_call" | custom-call | tf_op jit(solution)/shard_map/first/pallas_call | solution.py:684
  5.3 20.6 %sums.1.slots.old_slots = f32[32,4,8,128]{3,2,1,0:T(8,128)S(1)} custom-call(s32[256]{0:T(256)S(1)} %get-tuple-element.14.info, f32[32,8,128]{2,1,0:T(8,128)S(1)} %get-tuple-element.16.message), custom_call_target="tpu_custom_call" | custom-call | tf_op jit(solution)/shard_map/sums/pallas_call | solution.py:695
  25.9 0.0 copy-done
  25.9 4.0 %up.1.message = f32[32,8,128]{2,1,0:T(8,128)S(1)} custom-call(s32[256]{0:T(256)S(1)} %get-tuple-element.14.info, bf16[256,1024]{1,0:T(8,128)(2,1)S(1)} %get-tuple-element.15.hot, f32[1024,1024]{1,0:T(8,128)S(1)} %bitcast.3, f32[32,4,8,128]{3,2,1,0:T(8,128)S(1)} %sums.1.slots.old_slots), custom_call_target="tpu_custom_call" | custom-call | tf_op jit(solution)/shard_map/up/pallas_call | solution.py:704
  29.9 9.7 %root_sums.1.slots = f32[32,4,8,128]{3,2,1,0:T(8,128)S(1)} custom-call(s32[256]{0:T(256)S(1)} %get-tuple-element.14.info, f32[32,8,128]{2,1,0:T(8,128)S(1)} %up.1.message, f32[32,4,8,128]{3,2,1,0:T(8,128)S(1)} %sums.1.slots.old_slots), custom_call_target="tpu_custom_call" | custom-call | tf_op jit(solution)/shard_map/root_sums/pallas_call | solution.py:707
  39.6 2.4 %chain_1.1 = (f32[32,8,128]{2,1,0:T(8,128)S(1)}, f32[1024,1024]{1,0:T(8,128)S(1)}) custom-call(s32[256]{0:T(256)S(1)} %get-tuple-element.14.info, bf16[256,1024]{1,0:T(8,128)(2,1)S(1)} %get-tuple-element.15.hot, f32[1024,1024]{1,0:T(8,128)S(1)} %bitcast.4, f32[32,4,8,128]{3,2,1,0:T(8,128)S(1)} %root_sums.1.slots), custom_call_target="tpu_custom_call" | custom-call | tf_op jit(solution)/shard_map/chain_1/pallas_call | solution.py:728
  42.0 0.1 hop_1.1.arrived.first
  42.1 1.7 %chain_2.1.sent = f32[32,8,128]{2,1,0:T(8,128)S(1)} custom-call(s32[256]{0:T(256)S(1)} %get-tuple-element.14.info, bf16[256,1024]{1,0:T(8,128)(2,1)S(1)} %get-tuple-element.15.hot, f32[1024,1024]{1,0:T(8,128)S(1)} %get-tuple-element.17.table, f32[32,8,128]{2,1,0:T(8,128)S(1)} %hop_1.1.arrived.first), custom_call_target="tpu_custom_call" | custom-call | tf_op jit(solution)/shard_map/chain_2/pallas_call | solution.py:732
  43.8 0.1 hop_2.1.arrived
  44.0 1.5 %chain_3.1 = (f32[32,8,128]{2,1,0:T(8,128)S(1)}, f32[1024,1024]{1,0:T(8,128)S(1)}) custom-call(s32[256]{0:T(256)S(1)} %get-tuple-element.14.info, bf16[256,1024]{1,0:T(8,128)(2,1)S(1)} %get-tuple-element.15.hot, f32[1024,1024]{1,0:T(8,128)S(1)} %get-tuple-element.17.table, f32[32,8,128]{2,1,0:T(8,128)S(1)} %hop_2.1.arrived), custom_call_target="tpu_custom_call" | custom-call | tf_op jit(solution)/shard_map/chain_3/pallas_call | solution.py:741
  45.5 57.7 %down.1 = (f32[32,8,128]{2,1,0:T(8,128)S(1)}, f32[32,8,128]{2,1,0:T(8,128)S(1)}) custom-call(s32[256]{0:T(256)S(1)} %get-tuple-element.14.info, bf16[256,1024]{1,0:T(8,128)(2,1)S(1)} %get-tuple-element.15.hot, f32[1024,1024]{1,0:T(8,128)S(1)} %get-tuple-element.19.table, f32[32,8,128]{2,1,0:T(8,128)S(1)} %hop_1.1.arrived.first, ...), custom_call_target="tpu_custom_call" | custom-call | tf_op jit(solution)/shard_map/down/pallas_call | solution.py:749
  103.1 3.1 %final.1 = f32[1024,1024]{1,0:T(8,128)} custom-call(s32[256]{0:T(256)S(1)} %get-tuple-element.14.info, bf16[256,1024]{1,0:T(8,128)(2,1)S(1)} %get-tuple-element.15.hot, f32[1024,1024]{1,0:T(8,128)S(1)} %get-tuple-element.19.table, f32[32,8,128]{2,1,0:T(8,128)S(1)} %get-tuple-element.21.last_root, f32[32,8,128]{2,1,0:T(8,128)S(1)} %get-tuple-element.22.received, ...), custom_call_target="tpu_custom_call" | custom-call | tf_op jit(solution)/shard_map/final/pallas_call | solution.py:758
Async XLA Ops:
  0.0 25.9 %copy-start = (f32[1,1,1024,1024]{3,2,1,0:T(8,128)S(1)}, f32[1,1,1024,1024]{3,2,1,0:T(8,128)}, u32[]{:S(2)}) copy-start(f32[1,1,1024,1024]{3,2,1,0:T(8,128)} %param.4) | copy-start | bytes 12582916

commit v6 on v5

--- a/solution.py
+++ b/solution.py
@@ -565,7 +565,7 @@
             last_root[piece] = third[piece]
             return carry
 
-        lax.fori_loop(0, PIECES, body, 0)
+        lax.fori_loop(0, PIECES, body, 0, unroll=8)
 
     @pl.when(jnp.logical_not(receives))
     def _():
@@ -573,7 +573,7 @@
             last_root[piece] = first[piece]
             return carry
 
-        lax.fori_loop(0, PIECES, body, 0)
+        lax.fori_loop(0, PIECES, body, 0, unroll=8)
 
     @pl.when(me == 0)
     def _():
@@ -584,7 +584,7 @@
                 held[piece, k] = jnp.where(slot == k, last_root[piece], 0.0)
             return carry
 
-        lax.fori_loop(0, PIECES, body, 0)
+        lax.fori_loop(0, PIECES, body, 0, unroll=8)
         place_slots(table, belief, held, tools)
         send_margins(sems[0], from_root, ((2, 3), (1,), (0,)))
 
@@ -619,7 +619,7 @@
                 held[piece, k] = jnp.where(drop == k, value, 0.0)
             return carry
 
-        lax.fori_loop(0, PIECES, body, 0)
+        lax.fori_loop(0, PIECES, body, 0, unroll=8)
         place_slots(table, belief, held, tools)
         send_margins(sems[2], arrived.at[me], ((0,), (1,), (2, 3)))
         part_of(me, PIECES - 2, margins, arrived, sems[2]).wait_recv()

time: 107 us -> 106 us (level)
    pallas_call x1, Pallas kernels: 57.7 us -> 56 us  [per_device(): call(down_kernel, 'down', [S_SPEC] + [V_SPEC] * 5, (MESSAGE, MESSAGE), (V...]
where the time goes in v6:
time: 106 us
  Pallas kernels  105 us (99%)
    pallas_call x1, Pallas kernels, per_device(): call(down_kernel, 'down', [S_SPEC] + [V_SPEC] * 5, (MESSAGE, MESSAGE), (V...  56 us
    pallas_call x1, Pallas kernels, per_device(): call(sums_kernel, 'sums', [S_SPEC, V_SPEC], SLOTS, V_SPEC, [HELD_MESSAGE,...  21.3 us
    pallas_call x1, Pallas kernels, per_device(): call(root_sums_kernel, 'root_sums', [S_SPEC] + [V_SPEC] * 2, SLOTS, V_SPE...  10.2 us
    pallas_call x1, Pallas kernels, per_device(): call(first_kernel, 'first', [ANY_SPEC] * 2, (MESSAGE, jax.ShapeDtypeStruc...  3.93 us
    pallas_call x1, Pallas kernels, per_device(): call(up_kernel, 'up', [S_SPEC] + [V_SPEC] * 3, MESSAGE, V_SPEC, [HELD_TAB...  3.25 us
    pallas_call x1, Pallas kernels, per_device(): call(final_kernel, 'final', [S_SPEC] + [V_SPEC] * 5, TABLE, ANY_SPEC, [HE...  3.05 us
    pallas_call x1, Pallas kernels, per_device(): call(functools.partial(chain_kernel, 2), 'chain_2', [S_SPEC] + [V_SPEC] *...  2.41 us
    pallas_call x1, Pallas kernels, per_device(): call(chain_first_kernel, 'chain_1', [S_SPEC] + [V_SPEC] * 3, (MESSAGE, TA...  2.37 us

profile of v6, /device:TPU:1, one launch (start us, length us, event | category | flops | bytes accessed | tf_op | source)
XLA Modules:
  0.0 106.0 jit_solution(757221833780211432)
XLA Ops:
  0.0 0.0 copy-start
  0.0 0.9 pad_add_fusion.trees_in
  0.9 3.9 %first.1 = (f32[32,8,128]{2,1,0:T(8,128)S(1)}, s32[256]{0:T(256)S(1)}, bf16[256,1024]{1,0:T(8,128)(2,1)S(1)}) custom-call(s32[9,32]{1,0:T(8,128)S(1)} %pad_add_fusion.trees_in, f32[1024,1024]{1,0:T(8,128)} %bitcast.2), custom_call_target="tpu_custom_call" | custom-call | tf_op jit(solution)/shard_map/first/pallas_call | solution.py:684
  4.8 21.3 %sums.1.slots.old_slots = f32[32,4,8,128]{3,2,1,0:T(8,128)S(1)} custom-call(s32[256]{0:T(256)S(1)} %get-tuple-element.14.info, f32[32,8,128]{2,1,0:T(8,128)S(1)} %get-tuple-element.16.message), custom_call_target="tpu_custom_call" | custom-call | tf_op jit(solution)/shard_map/sums/pallas_call | solution.py:695
  26.1 0.0 copy-done
  26.1 3.3 %up.1.message = f32[32,8,128]{2,1,0:T(8,128)S(1)} custom-call(s32[256]{0:T(256)S(1)} %get-tuple-element.14.info, bf16[256,1024]{1,0:T(8,128)(2,1)S(1)} %get-tuple-element.15.hot, f32[1024,1024]{1,0:T(8,128)S(1)} %bitcast.3, f32[32,4,8,128]{3,2,1,0:T(8,128)S(1)} %sums.1.slots.old_slots), custom_call_target="tpu_custom_call" | custom-call | tf_op jit(solution)/shard_map/up/pallas_call | solution.py:704
  29.3 10.2 %root_sums.1.slots = f32[32,4,8,128]{3,2,1,0:T(8,128)S(1)} custom-call(s32[256]{0:T(256)S(1)} %get-tuple-element.14.info, f32[32,8,128]{2,1,0:T(8,128)S(1)} %up.1.message, f32[32,4,8,128]{3,2,1,0:T(8,128)S(1)} %sums.1.slots.old_slots), custom_call_target="tpu_custom_call" | custom-call | tf_op jit(solution)/shard_map/root_sums/pallas_call | solution.py:707
  39.5 2.4 %chain_1.1 = (f32[32,8,128]{2,1,0:T(8,128)S(1)}, f32[1024,1024]{1,0:T(8,128)S(1)}) custom-call(s32[256]{0:T(256)S(1)} %get-tuple-element.14.info, bf16[256,1024]{1,0:T(8,128)(2,1)S(1)} %get-tuple-element.15.hot, f32[1024,1024]{1,0:T(8,128)S(1)} %bitcast.4, f32[32,4,8,128]{3,2,1,0:T(8,128)S(1)} %root_sums.1.slots), custom_call_target="tpu_custom_call" | custom-call | tf_op jit(solution)/shard_map/chain_1/pallas_call | solution.py:728
  41.9 0.1 hop_1.1.arrived.first
  42.0 2.4 %chain_2.1.sent = f32[32,8,128]{2,1,0:T(8,128)S(1)} custom-call(s32[256]{0:T(256)S(1)} %get-tuple-element.14.info, bf16[256,1024]{1,0:T(8,128)(2,1)S(1)} %get-tuple-element.15.hot, f32[1024,1024]{1,0:T(8,128)S(1)} %get-tuple-element.17.table, f32[32,8,128]{2,1,0:T(8,128)S(1)} %hop_1.1.arrived.first), custom_call_target="tpu_custom_call" | custom-call | tf_op jit(solution)/shard_map/chain_2/pallas_call | solution.py:732
  44.5 0.1 hop_2.1.arrived
  44.6 2.2 %chain_3.1 = (f32[32,8,128]{2,1,0:T(8,128)S(1)}, f32[1024,1024]{1,0:T(8,128)S(1)}) custom-call(s32[256]{0:T(256)S(1)} %get-tuple-element.14.info, bf16[256,1024]{1,0:T(8,128)(2,1)S(1)} %get-tuple-element.15.hot, f32[1024,1024]{1,0:T(8,128)S(1)} %get-tuple-element.17.table, f32[32,8,128]{2,1,0:T(8,128)S(1)} %hop_2.1.arrived), custom_call_target="tpu_custom_call" | custom-call | tf_op jit(solution)/shard_map/chain_3/pallas_call | solution.py:741
  46.8 56.0 %down.1 = (f32[32,8,128]{2,1,0:T(8,128)S(1)}, f32[32,8,128]{2,1,0:T(8,128)S(1)}) custom-call(s32[256]{0:T(256)S(1)} %get-tuple-element.14.info, bf16[256,1024]{1,0:T(8,128)(2,1)S(1)} %get-tuple-element.15.hot, f32[1024,1024]{1,0:T(8,128)S(1)} %get-tuple-element.19.table, f32[32,8,128]{2,1,0:T(8,128)S(1)} %hop_1.1.arrived.first, ...), custom_call_target="tpu_custom_call" | custom-call | tf_op jit(solution)/shard_map/down/pallas_call | solution.py:749
  102.8 3.1 %final.1 = f32[1024,1024]{1,0:T(8,128)} custom-call(s32[256]{0:T(256)S(1)} %get-tuple-element.14.info, bf16[256,1024]{1,0:T(8,128)(2,1)S(1)} %get-tuple-element.15.hot, f32[1024,1024]{1,0:T(8,128)S(1)} %get-tuple-element.19.table, f32[32,8,128]{2,1,0:T(8,128)S(1)} %get-tuple-element.21.last_root, f32[32,8,128]{2,1,0:T(8,128)S(1)} %get-tuple-element.22.received, ...), custom_call_target="tpu_custom_call" | custom-call | tf_op jit(solution)/shard_map/final/pallas_call | solution.py:758
Async XLA Ops:
  0.0 26.1 %copy-start = (f32[1,1,1024,1024]{3,2,1,0:T(8,128)S(1)}, f32[1,1,1024,1024]{3,2,1,0:T(8,128)}, u32[]{:S(2)}) copy-start(f32[1,1,1024,1024]{3,2,1,0:T(8,128)} %param.4) | copy-start | bytes 12582916

commit v7 on v6

--- a/solution.py
+++ b/solution.py
@@ -215,7 +215,7 @@
                 across_2[block, 8 * m : 8 * (m + 1), :] = tops[m] + jnp.log(totals[m])
         return carry
 
-    lax.fori_loop(0, 8, body, 0, unroll=4)
+    lax.fori_loop(0, 8, body, 0, unroll=4 if put_2 and put_3 else 8)
     if put_2 is not None:
         put_turned(across_2, flat, put_2)
     if put_3 is not None:

time: 106 us -> 106 us (level)
    pallas_call x1, Pallas kernels: 56 us -> 57.4 us  [per_device(): call(down_kernel, 'down', [S_SPEC] + [V_SPEC] * 5, (MESSAGE, MESSAGE), (V...]
    pallas_call x1, Pallas kernels: 2.41 us -> 1.3 us  [per_device(): call(functools.partial(chain_kernel, 2), 'chain_2', [S_SPEC] + [V_SPEC] *...]
where the time goes in v7:
time: 106 us; the launch traced here: 105 us
  Pallas kernels  104 us (98%)
    pallas_call x1, Pallas kernels, per_device(): call(down_kernel, 'down', [S_SPEC] + [V_SPEC] * 5, (MESSAGE, MESSAGE), (V...  57.4 us
    pallas_call x1, Pallas kernels, per_device(): call(sums_kernel, 'sums', [S_SPEC, V_SPEC], SLOTS, V_SPEC, [HELD_MESSAGE,...  21.1 us
    pallas_call x1, Pallas kernels, per_device(): call(root_sums_kernel, 'root_sums', [S_SPEC] + [V_SPEC] * 2, SLOTS, V_SPE...  10.1 us
    pallas_call x1, Pallas kernels, per_device(): call(first_kernel, 'first', [ANY_SPEC] * 2, (MESSAGE, jax.ShapeDtypeStruc...  3.92 us
    pallas_call x1, Pallas kernels, per_device(): call(up_kernel, 'up', [S_SPEC] + [V_SPEC] * 3, MESSAGE, V_SPEC, [HELD_TAB...  3.25 us
    pallas_call x1, Pallas kernels, per_device(): call(final_kernel, 'final', [S_SPEC] + [V_SPEC] * 5, TABLE, ANY_SPEC, [HE...  3.05 us
    pallas_call x1, Pallas kernels, per_device(): call(chain_first_kernel, 'chain_1', [S_SPEC] + [V_SPEC] * 3, (MESSAGE, TA...  2.55 us

profile of v7, /device:TPU:1, one launch (start us, length us, event | category | flops | bytes accessed | tf_op | source)
XLA Modules:
  0.0 105.4 jit_solution(4867613208052362963)
XLA Ops:
  0.0 0.0 copy-start
  0.0 0.9 pad_add_fusion.trees_in
  0.9 3.9 %first.1 = (f32[32,8,128]{2,1,0:T(8,128)S(1)}, s32[256]{0:T(256)S(1)}, bf16[256,1024]{1,0:T(8,128)(2,1)S(1)}) custom-call(s32[9,32]{1,0:T(8,128)S(1)} %pad_add_fusion.trees_in, f32[1024,1024]{1,0:T(8,128)} %bitcast.2), custom_call_target="tpu_custom_call" | custom-call | tf_op jit(solution)/shard_map/first/pallas_call | solution.py:684
  4.8 21.1 %sums.1.slots.old_slots = f32[32,4,8,128]{3,2,1,0:T(8,128)S(1)} custom-call(s32[256]{0:T(256)S(1)} %get-tuple-element.14.info, f32[32,8,128]{2,1,0:T(8,128)S(1)} %get-tuple-element.16.message), custom_call_target="tpu_custom_call" | custom-call | tf_op jit(solution)/shard_map/sums/pallas_call | solution.py:695
  25.9 0.0 copy-done
  25.9 3.3 %up.1.message = f32[32,8,128]{2,1,0:T(8,128)S(1)} custom-call(s32[256]{0:T(256)S(1)} %get-tuple-element.14.info, bf16[256,1024]{1,0:T(8,128)(2,1)S(1)} %get-tuple-element.15.hot, f32[1024,1024]{1,0:T(8,128)S(1)} %bitcast.3, f32[32,4,8,128]{3,2,1,0:T(8,128)S(1)} %sums.1.slots.old_slots), custom_call_target="tpu_custom_call" | custom-call | tf_op jit(solution)/shard_map/up/pallas_call | solution.py:704
  29.1 10.1 %root_sums.1.slots = f32[32,4,8,128]{3,2,1,0:T(8,128)S(1)} custom-call(s32[256]{0:T(256)S(1)} %get-tuple-element.14.info, f32[32,8,128]{2,1,0:T(8,128)S(1)} %up.1.message, f32[32,4,8,128]{3,2,1,0:T(8,128)S(1)} %sums.1.slots.old_slots), custom_call_target="tpu_custom_call" | custom-call | tf_op jit(solution)/shard_map/root_sums/pallas_call | solution.py:707
  39.3 2.6 %chain_1.1 = (f32[32,8,128]{2,1,0:T(8,128)S(1)}, f32[1024,1024]{1,0:T(8,128)S(1)}) custom-call(s32[256]{0:T(256)S(1)} %get-tuple-element.14.info, bf16[256,1024]{1,0:T(8,128)(2,1)S(1)} %get-tuple-element.15.hot, f32[1024,1024]{1,0:T(8,128)S(1)} %bitcast.4, f32[32,4,8,128]{3,2,1,0:T(8,128)S(1)} %root_sums.1.slots), custom_call_target="tpu_custom_call" | custom-call | tf_op jit(solution)/shard_map/chain_1/pallas_call | solution.py:728
  41.9 0.1 hop_1.1.arrived.first
  42.0 1.3 %chain_2.1.sent = f32[32,8,128]{2,1,0:T(8,128)S(1)} custom-call(s32[256]{0:T(256)S(1)} %get-tuple-element.14.info, bf16[256,1024]{1,0:T(8,128)(2,1)S(1)} %get-tuple-element.15.hot, f32[1024,1024]{1,0:T(8,128)S(1)} %get-tuple-element.17.table, f32[32,8,128]{2,1,0:T(8,128)S(1)} %hop_1.1.arrived.first), custom_call_target="tpu_custom_call" | custom-call | tf_op jit(solution)/shard_map/chain_2/pallas_call | solution.py:732
  43.3 0.1 hop_2.1.arrived
  43.4 1.3 %chain_3.1 = (f32[32,8,128]{2,1,0:T(8,128)S(1)}, f32[1024,1024]{1,0:T(8,128)S(1)}) custom-call(s32[256]{0:T(256)S(1)} %get-tuple-element.14.info, bf16[256,1024]{1,0:T(8,128)(2,1)S(1)} %get-tuple-element.15.hot, f32[1024,1024]{1,0:T(8,128)S(1)} %get-tuple-element.17.table, f32[32,8,128]{2,1,0:T(8,128)S(1)} %hop_2.1.arrived), custom_call_target="tpu_custom_call" | custom-call | tf_op jit(solution)/shard_map/chain_3/pallas_call | solution.py:741
  44.7 57.4 %down.1 = (f32[32,8,128]{2,1,0:T(8,128)S(1)}, f32[32,8,128]{2,1,0:T(8,128)S(1)}) custom-call(s32[256]{0:T(256)S(1)} %get-tuple-element.14.info, bf16[256,1024]{1,0:T(8,128)(2,1)S(1)} %get-tuple-element.15.hot, f32[1024,1024]{1,0:T(8,128)S(1)} %get-tuple-element.19.table, f32[32,8,128]{2,1,0:T(8,128)S(1)} %hop_1.1.arrived.first, ...), custom_call_target="tpu_custom_call" | custom-call | tf_op jit(solution)/shard_map/down/pallas_call | solution.py:749
  102.2 3.1 %final.1 = f32[1024,1024]{1,0:T(8,128)} custom-call(s32[256]{0:T(256)S(1)} %get-tuple-element.14.info, bf16[256,1024]{1,0:T(8,128)(2,1)S(1)} %get-tuple-element.15.hot, f32[1024,1024]{1,0:T(8,128)S(1)} %get-tuple-element.19.table, f32[32,8,128]{2,1,0:T(8,128)S(1)} %get-tuple-element.21.last_root, f32[32,8,128]{2,1,0:T(8,128)S(1)} %get-tuple-element.22.received, ...), custom_call_target="tpu_custom_call" | custom-call | tf_op jit(solution)/shard_map/final/pallas_call | solution.py:758
Async XLA Ops:
  0.0 25.9 %copy-start = (f32[1,1,1024,1024]{3,2,1,0:T(8,128)S(1)}, f32[1,1,1024,1024]{3,2,1,0:T(8,128)}, u32[]{:S(2)}) copy-start(f32[1,1,1024,1024]{3,2,1,0:T(8,128)} %param.4) | copy-start | bytes 12582916
